TPU v7x, 32 devices: a whole 2x2x4 slice. The times are simulated.
32 devices in a mesh: dp: 16 (over z, x, core), tensor: 2 (over y).
Axes of the slice: x: 2, y: 2, z: 4, core: 2. Of those that a mesh axis runs over, the one named last changes fastest.
Arguments:
- hidden_in: bfloat16 [24576, 768], P(('dp', 'tensor')), may hold values from -6 to 6
- bounds: int32 [16, 6], P('dp'), may hold values from 0 to 1536, as said below
- attn_gain: float32 [768], replicated, may hold values from 0.1 to 1.9
- w_qkv: bfloat16 [3, 768, 768], P(None, None, 'tensor'), may hold values from -0.21875 to 0.21875
- w_attn: bfloat16 [768, 768], P('tensor'), may hold values from -3 to 3
- mlp_gain: float32 [768], replicated, may hold values from 0.1 to 1.9
- w_in: bfloat16 [2, 768, 1152], P(None, None, 'tensor'), may hold values from -0.21875 to 0.21875
- w_out: bfloat16 [1152, 768], P('tensor'), may hold values from -0.1875 to 0.1875
- cotangent: bfloat16 [24576, 768], P(('dp', 'tensor')), may hold values from -6 to 6
Outputs:
- hidden_out: bfloat16 [24576, 768], P(('dp', 'tensor'))
- grad_in: bfloat16 [24576, 768], P(('dp', 'tensor'))
- grad_attn_gain: float32 [768], replicated
- grad_w_qkv: float32 [3, 768, 768], P(None, None, 'tensor')
- grad_w_attn: float32 [768, 768], P('tensor')
- grad_mlp_gain: float32 [768], replicated
- grad_w_in: float32 [2, 768, 1152], P(None, None, 'tensor')
- grad_w_out: float32 [1152, 768], P('tensor')
Inputs may be any that keep to these rules, and one draw needn't show every extreme that they name: Each row of bounds holds 6 nondecreasing offsets into the 1536 slots of one index of dp, the first 0; consecutive offsets bound one sequence (some empty), slots from the last offset on are padding. In every row one sequence holds slots 1536 // 2 - 1 and 768; in some row a single sequence fills all 1536 slots.
All inputs are finite; a program needn't handle non-finite values.
Results may differ from a plain program's by a relative error of at most 0.015.
The roundings to bfloat16 on the way count: a program that leaves them out, or rounds other values in their place, can miss the bound.
Values may be sent and summed in bfloat16 or wider, within the bound.
No kernel may reach another device: no remote copies, remote signals or barrier semaphores. Data moves between devices by JAX's collectives and lax.ppermute only.
A program may use at most 192 MiB of HBM per device.

v0:
```python
import functools

import jax
import jax.numpy as jnp
import numpy as np
from jax import lax
from jax.experimental import pallas as pl
from jax.experimental.pallas import tpu as pltpu
from jax.sharding import PartitionSpec as P

HD = 64
NSEG = 6
PAIR = 2 * HD
BLK = 384
MLP_BLK = 256
COST = 0.15
KBLK = 512
rope_theta = 160000.0
norm_eps = 1e-05
masked_score = -1e30
f32 = jnp.float32
bf16 = jnp.bfloat16


def params(mib):
    return pltpu.CompilerParams(vmem_limit_bytes=mib * 1024 * 1024)


def cost(flops, nbytes):
    return pl.CostEstimate(
        flops=int(flops * COST), bytes_accessed=int(nbytes * COST), transcendentals=0
    )


def nn(a, b):
    return jnp.dot(a, b, preferred_element_type=f32)


def nt(a, b):
    return lax.dot_general(a, b, (((1,), (1,)), ((), ())), preferred_element_type=f32)


def call(body, args, deps=(), *, in_specs, **kw):
    first = len(in_specs)

    def run(*refs):
        body(*refs[:first], *refs[first + len(deps) :])

    return pl.pallas_call(
        run, in_specs=list(in_specs) + [pl.BlockSpec(memory_space=pl.ANY)] * len(deps), **kw
    )(*args, *deps)


def whole(shape):
    return pl.BlockSpec(shape, lambda i: (0,) * len(shape))


def unit_rows(x):
    centred = x - jnp.mean(x, axis=-1, keepdims=True)
    inv = lax.rsqrt(jnp.mean(centred * centred, axis=-1, keepdims=True) + norm_eps)
    return centred * inv, inv


def norm_back(e, xh, inv):
    return inv * (
        e - jnp.mean(e, axis=-1, keepdims=True) - xh * jnp.mean(e * xh, axis=-1, keepdims=True)
    )


def turn(x, cosine, sine, back):
    lane = lax.broadcasted_iota(jnp.int32, x.shape, 1) % HD
    other = jnp.where(lane < HD // 2, pltpu.roll(x, PAIR - HD // 2, 1), pltpu.roll(x, HD // 2, 1))
    return x * cosine - other * sine if back else x * cosine + other * sine


def sincos(x):
    turns = jnp.floor(x * 0.6366197723675814 + 0.5)
    r = ((x - turns * 1.5703125) - turns * 4.837512969970703125e-4) - turns * 7.54978995489188e-8
    z = r * r
    s = r + r * z * (-1.6666654611e-1 + z * (8.3321608736e-3 + z * -1.9515295891e-4))
    c = 1.0 - 0.5 * z + z * z * (
        4.166664568298827e-2 + z * (-1.388731625493765e-3 + z * 2.443315711809948e-5)
    )
    quarter = turns.astype(jnp.int32) & 3
    odd = (quarter & 1) == 1
    sine = jnp.where(odd, c, s)
    cosine = jnp.where(odd, s, c)
    sine = jnp.where(quarter >= 2, -sine, sine)
    cosine = jnp.where(jnp.logical_or(quarter == 1, quarter == 2), -cosine, cosine)
    return sine, cosine


def tables_body(edge_ref, first_ref, freq_ref, cos_ref, sin_ref, fq_ref, fk_ref):
    cap = cos_ref.shape[0]
    ids = lax.broadcasted_iota(jnp.int32, (cap, PAIR), 0) + first_ref[0]
    ids = jnp.where(ids >= cap, ids - cap, ids)
    lane = lax.broadcasted_iota(jnp.int32, ids.shape, 1)
    seg = jnp.zeros(ids.shape, jnp.int32)
    begin = jnp.zeros(ids.shape, jnp.int32)
    for n in range(1, NSEG):
        passed = ids >= edge_ref[0, n]
        seg = jnp.where(passed, seg + 1, seg)
        begin = jnp.where(passed, edge_ref[0, n], begin)
    angle = (ids - begin).astype(f32) * freq_ref[...]
    sine, cosine = sincos(angle)
    slot = lane % HD
    cos_ref[...] = cosine
    sin_ref[...] = jnp.where(slot < HD // 2, -sine, sine)
    same = slot == seg
    fq_ref[...] = jnp.where(same, 1.0, 0.0).astype(bf16)
    fk_ref[...] = jnp.where(
        slot < NSEG,
        jnp.where(same, 0.0, masked_score),
        jnp.where(slot < NSEG + 3, 1.0, 0.0),
    ).astype(bf16)


def tables(edges, first, cap):
    steps = 2.0 * (np.arange(PAIR) % (HD // 2)) / HD
    freq = jnp.asarray(np.exp(-steps * np.log(rope_theta))[None].astype(np.float32))
    smem = pl.BlockSpec(memory_space=pltpu.SMEM)
    table = lambda t: jax.ShapeDtypeStruct((cap, PAIR), t)
    return pl.pallas_call(
        tables_body,
        in_specs=[smem, smem, pl.BlockSpec(memory_space=pltpu.VMEM)],
        out_shape=[table(f32), table(f32), table(bf16), table(bf16)],
        compiler_params=params(8),
        cost_estimate=cost(80 * cap * PAIR, 3e6),
        name="tables",
    )(edges, first, freq)


def stack_body(a_ref, i_ref, u_ref, w_ref, out_ref, qkv_ref):
    at = a_ref.shape[0]
    units = u_ref.shape[0]
    width = w_ref.shape[2]
    out_ref[:at] = a_ref[...]
    for n in range(2):
        out_ref[at + n * units : at + (n + 1) * units] = i_ref[n]
    out_ref[at + 2 * units :] = u_ref[...]
    for n in range(3):
        turned = w_ref[n].T
        for pair in range(width // PAIR):
            to = (3 * pair + n) * PAIR
            qkv_ref[to : to + PAIR] = turned[pair * PAIR : (pair + 1) * PAIR]


def stack(w_attn, w_in_turned, w_out, w_qkv, deps=()):
    at, d = w_attn.shape
    rows = at + 3 * w_out.shape[0]
    vmem = pl.BlockSpec(memory_space=pltpu.VMEM)
    return call(
        stack_body,
        (w_attn, w_in_turned, w_out, w_qkv),
        deps,
        in_specs=[vmem] * 4,
        out_shape=[
            jax.ShapeDtypeStruct((rows, d), bf16),
            jax.ShapeDtypeStruct((3 * w_qkv.shape[2], d), bf16),
        ],
        compiler_params=params(12),
        cost_estimate=cost(1e8, 10e6),
        name="stack",
    )


def qkv_body(h_ref, gain_ref, w_ref, cos_ref, sin_ref, *refs):
    n1_ref, q_ref, k_ref, v_ref = refs[-4:]
    unit, inv = unit_rows(h_ref[...].astype(f32))
    n1 = (unit * gain_ref[...]).astype(bf16)
    n1_ref[...] = n1
    cosine, sine = cos_ref[...], sin_ref[...]
    width = w_ref.shape[2]
    for which, out, scale in ((0, q_ref, 0.125), (1, k_ref, 1.0)):
        full = nn(n1, w_ref[which])
        for at in range(0, width, PAIR):
            turned = turn(full[:, at : at + PAIR], cosine, sine, False).astype(bf16)
            if scale != 1.0:
                turned = (turned.astype(f32) * scale).astype(bf16)
            out[:, at : at + PAIR] = turned
    v_ref[...] = nn(n1, w_ref[2]).astype(bf16)


def qkv(h, gain, w, cosine, sine, first, held, deps=()):
    rows, d = h.shape
    cap, width = cosine.shape[0], w.shape[2]
    off = first // BLK
    by_row = lambda n: pl.BlockSpec((BLK, n), lambda i: (i + off, 0))
    shapes = [jax.ShapeDtypeStruct((cap, n), bf16) for n in (d, width, width, width)]
    return call(
        qkv_body,
        (h, gain, w, cosine, sine, *held),
        deps,
        grid=(rows // BLK,),
        in_specs=[
            pl.BlockSpec((BLK, d), lambda i: (i, 0)),
            whole((1, d)),
            whole(w.shape),
            by_row(PAIR),
            by_row(PAIR),
        ]
        + [pl.BlockSpec(memory_space=pl.ANY)] * len(held),
        out_specs=[by_row(d), by_row(width), by_row(width), by_row(width)],
        out_shape=shapes,
        input_output_aliases={5 + n: n for n in range(len(held))},
        compiler_params=params(14),
        cost_estimate=cost(2 * 2 * rows * d * 3 * width, 12e6),
        name="qkv",
    )


def assemble_body(at_ref, *refs):
    pieces, out_ref, sems = refs[:-2], refs[-2], refs[-1]
    copies = []
    for n, ref in enumerate(pieces):
        to = pl.ds(pl.multiple_of(at_ref[n], 8), ref.shape[0])
        copies.append(pltpu.make_async_copy(ref, out_ref.at[to], sems.at[n]))
        copies[-1].start()
    for copy in copies:
        copy.wait()


def assemble(at, pieces, shape, deps=()):
    anywhere = pl.BlockSpec(memory_space=pl.ANY)
    return call(
        assemble_body,
        (at, *pieces),
        deps,
        in_specs=[pl.BlockSpec(memory_space=pltpu.SMEM)] + [anywhere] * len(pieces),
        out_specs=pl.BlockSpec(memory_space=pltpu.VMEM),
        out_shape=jax.ShapeDtypeStruct(shape, bf16),
        scratch_shapes=[pltpu.SemaphoreType.DMA((len(pieces),))],
        compiler_params=params(8),
        cost_estimate=cost(1e6, 6e6),
        name="assemble",
    )


def lanes_of(head, shape):
    lane = lax.broadcasted_iota(jnp.int32, shape, 1)
    return (lane < HD) if head == 0 else (lane >= HD)


def attend_body(q_ref, k_ref, v_ref, fq_ref, fk_ref, *refs):
    o0_ref, o1_ref, qa_ref, qb_ref = refs[-4:]
    q, k, v, fq, fk = q_ref[...], k_ref[...], v_ref[...], fq_ref[...], fk_ref[...]
    v_turned = v.T
    rows = q.shape[0]
    line = lax.broadcasted_iota(jnp.int32, (PAIR, rows), 0)
    tag = jnp.zeros((PAIR, rows), f32)
    mixed = []
    for head in (0, 1):
        q_in = jnp.where(lanes_of(head, q.shape), q, fq)
        k_in = jnp.where(lanes_of(head, k.shape), k, fk)
        score = nt(k_in, q_in)
        top = jnp.max(score, axis=0, keepdims=True)
        expo = jnp.exp(score - top)
        total = jnp.sum(expo, axis=0, keepdims=True)
        at = head * HD
        mixed.append(nn(v_turned[at : at + HD], expo.astype(bf16)) * (1.0 / total))
        left = -(top + jnp.log(total))
        for part in range(3):
            head_bits = left.astype(bf16).astype(f32)
            left = left - head_bits
            tag = jnp.where(line == HD - at + NSEG + part, head_bits, tag)
    o = jnp.concatenate(mixed, axis=0).T.astype(bf16)
    tag = tag.T
    fq = fq.astype(f32) + tag
    wide = q.astype(f32)
    qa_ref[...] = jnp.where(lanes_of(0, q.shape), wide, fq).astype(bf16)
    qb_ref[...] = jnp.where(lanes_of(1, q.shape), wide, fq).astype(bf16)

    @pl.when(pl.program_id(0) == 0)
    def _():
        o0_ref[...] = o

    @pl.when(pl.program_id(0) == 1)
    def _():
        o1_ref[...] = o


def attend(pair, q, k, v, feat_q, feat_k, held):
    cap, width = q.shape
    rows = cap // 2
    part = pl.BlockSpec((rows, PAIR), lambda i: (i, 0))
    full = pl.BlockSpec((cap, PAIR), lambda i: (0, pair))
    column = lambda n: pl.BlockSpec((rows, PAIR), lambda i: (0, n))
    far = width - PAIR if pair < 2 else PAIR
    return pl.pallas_call(
        attend_body,
        grid=(2,),
        in_specs=[
            pl.BlockSpec((rows, PAIR), lambda i: (i, pair)),
            full,
            full,
            part,
            whole((cap, PAIR)),
        ]
        + [pl.BlockSpec(memory_space=pl.ANY)] * len(held),
        out_specs=[column(pair), column(pair % 2)] + [part] * 2,
        out_shape=[
            jax.ShapeDtypeStruct((rows, width), bf16),
            jax.ShapeDtypeStruct((rows, far), bf16),
        ]
        + [jax.ShapeDtypeStruct((cap, PAIR), bf16)] * 2,
        input_output_aliases={5 + n: n for n in range(len(held))},
        compiler_params=params(12),
        cost_estimate=cost(2 * 2 * 2 * cap * cap * 256 * 2, 3e6),
        name="attend",
    )(q, k, v, feat_q, feat_k, *held)


def back_body(
    qa_ref, qb_ref, q_ref, k_ref, v_ref, fk_ref, o0_ref, o1_ref, d0_ref, d1_ref, cos_ref, sin_ref,
    out_ref, dol_ref, da_ref, db_ref, dqt_ref,
):
    step = pl.program_id(0)
    half = d0_ref.shape[0]
    cap = 2 * half

    @pl.when(step == 0)
    def _():
        dol_ref[:half] = d0_ref[...]
        dol_ref[half:] = d1_ref[...]
        dol = dol_ref[...]
        slot = lax.broadcasted_iota(jnp.int32, dol.shape, 1) % HD
        wide = dol.astype(f32)
        prod = wide * jnp.concatenate([o0_ref[...], o1_ref[...]], axis=0).astype(f32)
        for head, out in ((0, da_ref), (1, db_ref)):
            mine = lanes_of(head, dol.shape)
            left = -jnp.sum(jnp.where(mine, prod, 0.0), axis=-1, keepdims=True)
            tagged = jnp.where(mine, wide, 0.0)
            for part in range(3):
                head_bits = left.astype(bf16).astype(f32)
                left = left - head_bits
                tagged = jnp.where(
                    jnp.logical_and(jnp.logical_not(mine), slot == NSEG + part), head_bits, tagged
                )
            out[...] = tagged.astype(bf16)
        dqt_ref[...] = jnp.zeros_like(dqt_ref)

    k, v, fk, q, dol = k_ref[...], v_ref[...], fk_ref[...], q_ref[...], dol_ref[...]
    k_turned = k.T
    slot = lax.broadcasted_iota(jnp.int32, v.shape, 1) % HD
    ones = jnp.where(
        jnp.logical_and(slot >= NSEG, slot < NSEG + 3), 1.0, 0.0
    ).astype(bf16)
    dks, dvs = [], []
    for head, qe_ref, de_ref in ((0, qa_ref, da_ref), (1, qb_ref, db_ref)):
        mine = lanes_of(head, k.shape)
        probs = jnp.exp(nt(jnp.where(mine, k, fk), qe_ref[...]))
        dvs.append(nn(probs.astype(bf16), dol))
        ds = (probs * nt(jnp.where(mine, v, ones), de_ref[...])).astype(bf16)
        dks.append(nn(ds, q))
        at = head * HD
        dqt_ref[at : at + HD] += nn(k_turned[at : at + HD], ds)
    first = lanes_of(0, k.shape)
    rows = pl.ds(pl.multiple_of(step * KBLK, KBLK), KBLK)
    dk = jnp.where(first, dks[0], dks[1])
    out_ref[rows, PAIR : 2 * PAIR] = turn(dk, cos_ref[rows], sin_ref[rows], True).astype(bf16)
    out_ref[rows, 2 * PAIR :] = jnp.where(first, dvs[0], dvs[1]).astype(bf16)

    @pl.when(step == cap // KBLK - 1)
    def _():
        dq = dqt_ref[...].T * 0.125
        out_ref[:, :PAIR] = turn(dq, cos_ref[...], sin_ref[...], True).astype(bf16)


def attend_back(pair, qa, qb, q, k, v, feat_k, o0, o1, d0, d1, cosine, sine, deps=()):
    cap = q.shape[0]
    full = whole((cap, PAIR))
    block = pl.BlockSpec((KBLK, PAIR), lambda i: (i, pair))
    part = pl.BlockSpec((KBLK, PAIR), lambda i: (i, 0))
    column = lambda n: pl.BlockSpec((cap // 2, PAIR), lambda i: (0, n))
    return call(
        back_body,
        (qa, qb, q, k, v, feat_k, o0, o1, d0, d1, cosine, sine,),
        deps,
        grid=(cap // KBLK,),
        in_specs=[
            full,
            full,
            pl.BlockSpec((cap, PAIR), lambda i: (0, pair)),
            block,
            block,
            part,
            column(pair),
            column(pair % 2),
            column(pair),
            column(pair % 2),
            full,
            full,
        ],
        out_specs=whole((cap, 3 * PAIR)),
        out_shape=jax.ShapeDtypeStruct((cap, 3 * PAIR), bf16),
        scratch_shapes=[
            pltpu.VMEM((cap, PAIR), bf16),
            pltpu.VMEM((cap, PAIR), bf16),
            pltpu.VMEM((cap, PAIR), bf16),
            pltpu.VMEM((PAIR, cap), f32),
        ],
        compiler_params=params(58),
        cost_estimate=cost(5 * 2 * 2 * cap * cap * 256 * 2, 6e6),
        name="attend_back",
    )


def mlp_body(
    sc_ref, h_ref, cot_ref, oa_ref, ob01, ob2, gain_ref, own_ref, got_ref,
    out_ref, n2_ref, ga_ref, dx_ref, gm_ref, unit_ref, da_ref, db01, db2, gg_ref,
):
    step = pl.program_id(0)
    oa = oa_ref[...]
    ob = jnp.concatenate([ob01[...], ob2[...]], axis=1)
    width = oa.shape[1]
    units = unit_ref.shape[2]
    in0 = slice(width, width + units)
    in1 = slice(width + units, width + 2 * units)
    up = slice(width + 2 * units, width + 3 * units)
    x1 = h_ref[...].astype(f32) + (nn(oa, own_ref[:width]) + nn(ob, got_ref[:width]))
    xh, inv = unit_rows(x1)
    gain = gain_ref[...]
    n2 = (xh * gain).astype(bf16)
    n2_ref[...] = n2
    ids = sc_ref[0] + step * MLP_BLK + lax.broadcasted_iota(jnp.int32, x1.shape, 0)
    g = jnp.where(ids < sc_ref[1], cot_ref[...].astype(f32), 0.0)
    gm = g.astype(bf16)
    gm_ref[...] = gm
    m = jnp.zeros_like(x1)
    dn2 = jnp.zeros_like(x1)
    for n, w_ref in enumerate((own_ref, got_ref)):
        act = nt(n2, w_ref[in0])
        gate = nt(n2, w_ref[in1])
        phi = 0.5 * (1.0 + lax.erf(act * 0.7071067811865476))
        bell = jnp.exp(-0.5 * act * act) * 0.3989422804014327
        gelu = act * phi
        hidden = (gelu * gate).astype(bf16)
        unit_ref[3 * n + 2] = hidden
        m = m + nn(hidden, w_ref[up])
        dh = nt(gm, w_ref[up])
        dact = (dh * gate * (phi + act * bell)).astype(bf16)
        dgate = (dh * gelu).astype(bf16)
        unit_ref[3 * n] = dact
        unit_ref[3 * n + 1] = dgate
        dn2 = dn2 + nn(dact, w_ref[in0]) + nn(dgate, w_ref[in1])
    out_ref[...] = (x1 + m).astype(bf16)

    @pl.when(step == 0)
    def _():
        gg_ref[...] = jnp.zeros_like(gg_ref)

    gg_ref[...] += jnp.sum((dn2 * xh).reshape(-1, 8, x1.shape[1]), axis=0)
    dx = g + norm_back(dn2 * gain, xh, inv)
    dx_ref[...] = dx
    ga = dx.astype(bf16)
    ga_ref[...] = ga
    da_ref[...] = nt(ga, own_ref[:width]).astype(bf16)
    db = nt(ga, got_ref[:width]).astype(bf16)
    db01[...] = db[:, : 2 * PAIR]
    db2[...] = db[:, 2 * PAIR :]


def mlp(scalars, h, cot, o_own, o_got, gain, w_own, w_got, units, deps=()):
    rows, d = h.shape
    row = lambda n: pl.BlockSpec((MLP_BLK, n), lambda i: (i, 0))
    out = lambda n, t=bf16: jax.ShapeDtypeStruct((rows, n), t)
    return call(
        mlp_body,
        (scalars, h, cot, o_own, *o_got, gain, w_own, w_got),
        deps,
        grid=(rows // MLP_BLK,),
        in_specs=[pl.BlockSpec(memory_space=pltpu.SMEM), row(d), row(d)]
        + [row(3 * PAIR), row(2 * PAIR), row(PAIR)]
        + [whole((1, d))]
        + [whole(w_own.shape)] * 2,
        out_specs=[row(d)] * 5
        + [pl.BlockSpec((6, MLP_BLK, units), lambda i: (0, i, 0))]
        + [row(3 * PAIR), row(2 * PAIR), row(PAIR)]
        + [whole((8, d))],
        out_shape=[out(d), out(d), out(d), out(d, f32), out(d)]
        + [jax.ShapeDtypeStruct((6, rows, units), bf16)]
        + [out(3 * PAIR), out(2 * PAIR), out(PAIR)]
        + [jax.ShapeDtypeStruct((8, d), f32)],
        compiler_params=params(26),
        cost_estimate=cost(2 * 2 * 4 * rows * w_own.size, 24e6),
        name="mlp",
    )


def tn(a, b):
    return lax.dot_general(a, b, (((0,), (0,)), ((), ())), preferred_element_type=f32)


def grads_body(
    side, many, core_ref, *refs
):
    outs, unit_ref = refs[:many], refs[many]
    n2_ref, ga_ref, gm_ref, keep_ref, send_ref, held_ref, sems = refs[many + 1 :]
    core = core_ref[0]
    half = keep_ref.shape[0]
    n2, ga, gm = n2_ref[...], ga_ref[...], gm_ref[...]
    parts = [(x[...], ga) for x in outs]
    parts += [(unit_ref[n], n2 if n < 2 else gm) for n in range(3)]
    at = 0
    for left, right in parts:
        res = tn(left, right).astype(bf16)
        held_ref[at : at + res.shape[0]] = res
        at += res.shape[0]
    copies = []
    for out, which in ((keep_ref, core), (send_ref, 1 - core)):
        rows = pl.ds(pl.multiple_of(which * half, 16), half)
        copies.append(pltpu.make_async_copy(held_ref.at[rows], out, sems.at[len(copies)]))
        copies[-1].start()
    for copy in copies:
        copy.wait()


def weight_grads(side, core, o, by_unit, n2, ga, gm, deps=()):
    rows, d = n2.shape
    units = by_unit.shape[2]
    total = 3 * PAIR + 3 * units
    shape = jax.ShapeDtypeStruct((total // 2, d), bf16)
    vmem = pl.BlockSpec(memory_space=pltpu.VMEM)
    anywhere = pl.BlockSpec(memory_space=pl.ANY)
    return call(
        functools.partial(grads_body, side, len(o)),
        (core, *o, by_unit, n2, ga, gm),
        deps,
        grid=(1,),
        in_specs=[pl.BlockSpec(memory_space=pltpu.SMEM)]
        + [whole(x.shape) for x in o]
        + [pl.BlockSpec((3, rows, units), lambda i: (side, 0, 0))]
        + [whole((rows, d))] * 3,
        out_specs=[anywhere] * 2,
        out_shape=[shape] * 2,
        scratch_shapes=[pltpu.VMEM((total, d), bf16), pltpu.SemaphoreType.DMA((2,))],
        compiler_params=params(18),
        cost_estimate=cost(2 * 2 * rows * d * total, 9e6),
        name="weight_grads",
    )


def pair_body(core_ref, back_ref, n1_ref, keep_ref, send_ref, held_ref, sems):
    half = keep_ref.shape[0]
    held_ref[...] = tn(back_ref[...], n1_ref[...]).astype(bf16)
    copies = []
    for out, which in ((keep_ref, core_ref[0]), (send_ref, 1 - core_ref[0])):
        rows = pl.ds(pl.multiple_of(which * half, 16), half)
        copies.append(pltpu.make_async_copy(held_ref.at[rows], out, sems.at[len(copies)]))
        copies[-1].start()
    for copy in copies:
        copy.wait()


def pair_grads(core, back, n1, deps=()):
    cap, d = n1.shape
    shape = jax.ShapeDtypeStruct((3 * PAIR // 2, d), bf16)
    vmem = pl.BlockSpec(memory_space=pltpu.VMEM)
    anywhere = pl.BlockSpec(memory_space=pl.ANY)
    return call(
        pair_body,
        (core, back, n1,),
        deps,
        in_specs=[pl.BlockSpec(memory_space=pltpu.SMEM)] + [vmem] * 2,
        out_specs=[anywhere] * 2,
        out_shape=[shape] * 2,
        scratch_shapes=[pltpu.VMEM((3 * PAIR, d), bf16), pltpu.SemaphoreType.DMA((2,))],
        compiler_params=params(10),
        cost_estimate=cost(2 * 2 * cap * d * 3 * PAIR, 5e6),
        name="pair_grads",
    )


def unstack_body(core_ref, mine_ref, got_ref, a_ref, i_ref, u_ref):
    first = core_ref[0] == 0
    mine, got = mine_ref[...], got_ref[...]
    full = jnp.concatenate([jnp.where(first, mine, got), jnp.where(first, got, mine)], axis=0)
    at, units = a_ref.shape[0], u_ref.shape[0]
    a_ref[...] = full[:at].astype(f32)
    for n in range(2):
        i_ref[n] = full[at + n * units : at + (n + 1) * units].astype(f32)
    u_ref[...] = full[at + 2 * units :].astype(f32)


def unstack(core, mine, got, width, units, deps=()):
    d = mine.shape[1]
    vmem = pl.BlockSpec(memory_space=pltpu.VMEM)
    return call(
        unstack_body,
        (core, mine, got,),
        deps,
        in_specs=[pl.BlockSpec(memory_space=pltpu.SMEM), vmem, vmem],
        out_shape=[
            jax.ShapeDtypeStruct((width, d), f32),
            jax.ShapeDtypeStruct((2, units, d), f32),
            jax.ShapeDtypeStruct((units, d), f32),
        ],
        compiler_params=params(20),
        cost_estimate=cost(1e8, 10e6),
        name="unstack",
    )


def unpair_body(core_ref, mine_ref, got_ref, out_ref):
    first = core_ref[0] == 0
    half = mine_ref.shape[0] // 3
    for pair in range(3):
        rows = slice(pair * half, (pair + 1) * half)
        mine, got = mine_ref[rows], got_ref[rows]
        full = jnp.concatenate([jnp.where(first, mine, got), jnp.where(first, got, mine)], axis=0)
        for n in range(3):
            turned = full[n * PAIR : (n + 1) * PAIR].T.astype(f32)
            out_ref[n, :, pair * PAIR : (pair + 1) * PAIR] = turned


def unpair(core, mine, got, deps=()):
    d = mine.shape[1]
    vmem = pl.BlockSpec(memory_space=pltpu.VMEM)
    return call(
        unpair_body,
        (core, mine, got,),
        deps,
        in_specs=[pl.BlockSpec(memory_space=pltpu.SMEM), vmem, vmem],
        out_shape=jax.ShapeDtypeStruct((3, d, 3 * PAIR), f32),
        compiler_params=params(14),
        cost_estimate=cost(1e8, 6e6),
        name="unpair",
    )


def combine_body(side_ref, k0, c0, k1, c1, own_ref, far_ref, mine_ref, other_ref):
    low = side_ref[0] == 0
    head = own_ref.shape[0]
    half = mine_ref.shape[1]
    for n, (keep, came, out) in enumerate(((k0, c0, own_ref), (k1, c1, far_ref))):
        total = (keep[...].astype(f32) + came[...].astype(f32)).astype(bf16)
        out[...] = total[:head]
        first, second = total[head : head + half], total[head + half :]
        mine_ref[n] = jnp.where(low, first, second)
        other_ref[n] = jnp.where(low, second, first)


def combine(side, keep0, came0, keep1, came1, head, deps=()):
    rows, d = keep0.shape
    half = (rows - head) // 2
    vmem = pl.BlockSpec(memory_space=pltpu.VMEM)
    cut = jax.ShapeDtypeStruct((2, half, d), bf16)
    return call(
        combine_body,
        (side, keep0, came0, keep1, came1),
        deps,
        in_specs=[pl.BlockSpec(memory_space=pltpu.SMEM)] + [vmem] * 4,
        out_shape=[jax.ShapeDtypeStruct((head, d), bf16)] * 2 + [cut] * 2,
        compiler_params=params(20),
        cost_estimate=cost(4 * rows * d, 12e6),
        name="combine",
    )


def tail_body(
    b0, b1, b2, w_ref, h_ref, dn_ref, gg_ref
):
    dn = nn(jnp.concatenate([b0[...], b1[...], b2[...]], axis=1), w_ref[...])
    dn_ref[...] = dn.astype(dn_ref.dtype)
    xh, unused = unit_rows(h_ref[...].astype(f32))

    @pl.when(pl.program_id(0) == 0)
    def _():
        gg_ref[...] = jnp.zeros_like(gg_ref)

    gg_ref[...] += jnp.sum((dn * xh).reshape(-1, 8, dn.shape[1]), axis=0)


def tail(parts, w, h, first, dtype, deps=()):
    rows, d = h.shape
    off = first // BLK
    part = pl.BlockSpec((BLK, 3 * PAIR), lambda i: (i + off, 0))
    row = pl.BlockSpec((BLK, d), lambda i: (i, 0))
    return call(
        tail_body,
        (*parts, w, h,),
        deps,
        grid=(rows // BLK,),
        in_specs=[part] * 3 + [whole(w.shape), row],
        out_specs=[row, whole((8, d))],
        out_shape=[
            jax.ShapeDtypeStruct((rows, d), dtype),
            jax.ShapeDtypeStruct((8, d), f32),
        ],
        compiler_params=params(14),
        cost_estimate=cost(2 * 2 * rows * w.size, 8e6),
        name="tail",
    )


def last_body(h_ref, gain_ref, own_ref, got_ref, dx_ref, out_ref):
    xh, inv = unit_rows(h_ref[...].astype(f32))
    dn = own_ref[...] + got_ref[...].astype(f32)
    out_ref[...] = (dx_ref[...] + norm_back(dn * gain_ref[...], xh, inv)).astype(bf16)


def last(h, gain, own, got, dx, deps=()):
    rows, d = h.shape
    row = pl.BlockSpec((BLK, d), lambda i: (i, 0))
    return call(
        last_body,
        (h, gain, own, got, dx,),
        deps,
        grid=(rows // BLK,),
        in_specs=[row, whole((1, d)), row, row, row],
        out_specs=row,
        out_shape=jax.ShapeDtypeStruct((rows, d), bf16),
        compiler_params=params(12),
        cost_estimate=cost(40 * rows * d, 9e6),
        name="last",
    )


def on_device(dp, hidden_in, bounds, attn_gain, w_qkv, w_attn, mlp_gain, w_in, w_out, cotangent):
    rows, d = hidden_in.shape
    cap = 2 * rows
    width = w_attn.shape[0]
    units = w_out.shape[0]
    shard = lax.axis_index("tensor")
    place = lax.axis_index("dp")
    core = place % 2
    core_at = core.astype(jnp.int32).reshape(1)
    side = (place // 2) % 2
    groups = [list(range(c, dp, 2)) for c in range(2)]
    bits = [1 << n for n in range(dp.bit_length() - 1)]

    def over_y(x):
        return lax.ppermute(x, "tensor", [(0, 1), (1, 0)])

    def over(x, bit):
        return lax.ppermute(x, "dp", [(n, n ^ bit) for n in range(dp)])

    def over_core(x):
        return over(x, 1)

    def add(a, b):
        return (a.astype(f32) + b.astype(f32)).astype(bf16)

    def in_order(first, mine, got):
        return jnp.concatenate(
            [jnp.where(first, mine, got), jnp.where(first, got, mine)], axis=0
        )

    hidden_got = over_y(hidden_in)
    cosine, sine, feat_q, feat_k = tables(
        bounds, (shard * rows).astype(jnp.int32).reshape(1), cap
    )
    gain_a = attn_gain.reshape(1, d)
    gain_m = mlp_gain.reshape(1, d)
    held = qkv(hidden_in, gain_a, w_qkv, cosine, sine, 0, ())
    w_own, w_qkv_turned = stack(w_attn, jnp.swapaxes(w_in, 1, 2), w_out, w_qkv)
    quarter = w_own.shape[0] // 4
    piece = lax.dynamic_slice_in_dim(w_own, (2 * core + side) * quarter, quarter, 0)
    hidden_got, piece, held = lax.optimization_barrier((hidden_got, piece, held))
    n1, q, k, v = qkv(hidden_got, gain_a, w_qkv, cosine, sine, rows, held)

    def after(x, *done):
        return lax.optimization_barrier((x, done))[0]

    cut = (quarter // 2 + 15) // 16 * 16
    cuts = (piece[:cut], piece[cut:])
    from_y = [over_y(x) for x in cuts]
    first = attend(0, q, k, v, feat_q, feat_k, ())
    from_x = [over(after(from_y[0], first[0]), 2)]
    second = attend(1, q, k, v, feat_q, feat_k, first[:2])
    from_x.append(over(after(from_y[1], second[0]), 2))
    third = attend(2, q, k, v, feat_q, feat_k, second[:1])
    o_got = [over_y(second[1]), over_y(third[1])]
    pieces = [from_y[0], from_x[0], over_core(from_y[0]), over_core(after(from_x[0], second[0]))]
    pieces += [from_y[1], from_x[1], over_core(from_y[1]), over_core(after(from_x[1], third[0]))]
    at = jnp.arange(2, dtype=jnp.int32)[:, None] * cut + jnp.stack(
        [(2 * c + s) * quarter for c in (core, 1 - core) for s in (side, 1 - side)]
    )
    o_own = third[0]
    o_far = (second[1], second[1], third[1])
    q_tag = [x[2:] for x in (first, second, third)]
    w_got = assemble(at.reshape(8), pieces, w_own.shape, (o_got[0],))
    scalars = jnp.stack([shard * rows, bounds[0, NSEG - 1]]).astype(jnp.int32)
    (
        hidden_out, n2, ga, dx, gm, by_unit, d_own, db01, db2, gg_mlp,
    ) = mlp(scalars, hidden_in, cotangent, o_own, o_got, gain_m, w_own, w_got, units)
    d_got = [over_y(db01), over_y(db2)]
    d_far = (d_got[0], d_got[0], d_got[1])

    def back(pair, *deps):
        out = attend_back(
            pair, *q_tag[pair], q, k, v, feat_k, o_own, o_far[pair], d_own, d_far[pair],
            cosine, sine, deps,
        )
        return out

    def pair_sum(out, *deps):
        keep, send = pair_grads(core_at, out, n1, deps)
        return add(keep, over_core(send))

    def split(x, bit):
        low = (place & bit) == 0
        half = x.shape[0] // 2
        first, second = x[:half], x[half:]
        return jnp.where(low, first, second), jnp.where(low, second, first)

    def merge(x, bit):
        return in_order((place & bit) == 0, x, over(x, bit))

    def over_rest(x):
        if len(bits) < 3:
            return x
        mine, other = split(x, bits[2])
        mine = add(mine, over(other, bits[2]))
        for bit in bits[3:]:
            mine = add(mine, over(mine, bit))
        return merge(mine, bits[2])

    keep1, send1 = weight_grads(1, core_at, o_got, by_unit, n2, ga, gm)
    keep0, send0 = weight_grads(0, core_at, (o_own,), by_unit, n2, ga, gm, (keep1, d_got[0]))
    came1 = over_core(after(send1, d_got[0]))
    came0 = over_core(send0)
    head = send0.shape[0] // 32 * 16 - 16
    own_a, far_a, mine_b, other_b = combine(
        side.astype(jnp.int32).reshape(1), keep0, came0, keep1, came1, head
    )
    got_a, got_b = over_y(far_a), over(other_b, 2)
    back0 = back(0, mine_b, far_a)
    keep, send = pair_grads(core_at, back0, n1)
    pair0 = add(keep, over_core(send))

    own_a = add(own_a, after(got_a, back0))
    mine_b = add(mine_b, after(got_b, back0))
    mine_a, other_a = split(own_a, 2)
    got_a, got_b = over(other_a, 2), over_y(mine_b[1])
    back1 = back(1, keep, mine_a, mine_b)
    keep, send = pair_grads(core_at, back1, n1)
    pair1 = add(keep, over_core(send))

    got_a, got_b = after((got_a, got_b), back1)
    mine = jnp.concatenate([add(mine_a, got_a), add(mine_b[0], got_b)], axis=0)
    if len(bits) > 2:
        mine, other = split(mine, bits[2])
        got = over(other, bits[2])
    back2 = back(2, keep, mine)
    if len(bits) > 2:
        mine = add(mine, after(got, back2))
    parts = (back0, back1, back2)
    dn_other, gg_other = tail(parts, w_qkv_turned, hidden_got, rows, bf16, (mine,))
    dn_got = over_y(dn_other)
    keep, send = pair_grads(core_at, back2, n1, (dn_other,))
    pair2 = add(keep, over_core(send))
    dn_own, gg_own = tail(parts, w_qkv_turned, hidden_in, 0, f32, (keep,))

    if len(bits) > 2:
        for bit in bits[3:]:
            mine = add(mine, over(mine, bit))
        mine = merge(mine, bits[2])
    grad_in = last(hidden_in, gain_a, dn_own, dn_got, dx)
    got = over(after(mine, grad_in), 2)
    low = (place & 2) == 0
    grads = jnp.concatenate(
        [in_order(low, mine[: head // 2], got[: head // 2]),
         in_order(low, mine[head // 2 :], got[head // 2 :])],
        axis=0,
    )

    gains = jnp.stack(
        [jnp.sum(gg_own, axis=0) + jnp.sum(gg_other, axis=0), jnp.sum(gg_mlp, axis=0)]
    )
    gains = gains + over_core(gains)
    gains = gains + over(gains, 2)
    gains = jnp.pad(gains, ((0, 14), (0, 0))).astype(bf16)
    mine, other = split(jnp.concatenate([pair0, pair1, pair2], axis=0), 2)
    mine = add(mine, over(other, 2))
    count = mine.shape[0]
    mine = over_rest(jnp.concatenate([mine, gains], axis=0))
    gains = mine[count : count + 2].astype(f32)
    gains = gains + over_y(gains)
    pairs = merge(mine[:count], 2)

    grad_w_attn, grad_w_in, grad_w_out = unstack(core_at, grads, over_core(grads), width, units)
    grad_w_in = jnp.swapaxes(grad_w_in, 1, 2)
    grad_w_qkv = unpair(core_at, pairs, over_core(pairs))
    return (
        hidden_out,
        grad_in,
        gains[0],
        grad_w_qkv,
        grad_w_attn,
        gains[1],
        grad_w_in,
        grad_w_out,
    )


def solution(mesh):
    in_specs = (
        P(("dp", "tensor"), None),
        P("dp", None),
        P(),
        P(None, None, "tensor"),
        P("tensor", None),
        P(),
        P(None, None, "tensor"),
        P("tensor", None),
        P(("dp", "tensor"), None),
    )
    out_specs = (
        P(("dp", "tensor"), None),
        P(("dp", "tensor"), None),
        P(),
        P(None, None, "tensor"),
        P("tensor", None),
        P(),
        P(None, None, "tensor"),
        P("tensor", None),
    )
    return jax.shard_map(
        functools.partial(on_device, mesh.shape["dp"]),
        mesh=mesh,
        in_specs=in_specs,
        out_specs=out_specs,
        check_vma=False,
    )
```

profile of v0, /device:TPU:0, one launch (start us, length us, event | category | flops | bytes accessed | tf_op | source)
XLA Modules:
  0.0 304.9 jit_solution(16240725318875887426)
XLA Ops:
  0.6 3.0 collective-permute-start
  16.6 3.0 qkv.2
  19.8 10.2 %collective-permute-done.refs_0_.refs_4_ = bf16[768,768]{1,0:T(8,128)(2,1)} collective-permute-done((bf16[768,768]{1,0:T(8,128)(2,1)}, bf16[768,768]{1,0:T(8,128)(2,1)}, u32[]{:S(2)}, u32[]{:S(2)}) %collective-permute-start) | collective-permute-done | bytes 1179680 | tf_op jit(solution)/shard_map/ppermute | solution.py:733
  32.2 3.8 %qkv.3 = (bf16[1536,768]{1,0:T(8,128)(2,1)S(1)}, bf16[1536,384]{1,0:T(8,128)(2,1)S(1)}, bf16[1536,384]{1,0:T(8,128)(2,1)S(1)}, bf16[1536,384]{1,0:T(8,128)(2,1)S(1)}) custom-call(bf16[768,768]{1,0:T(8,128)(2,1)} %collective-permute-done.refs_0_.refs_4_, ...), custom_call_target="tpu_custom_call", output_to_operand_aliasing={{0}: (5, {}), {1}: (6, {}), {2}: (7, {}), {3}: (8, {})} | custom-call | flops 407686336 | bytes 1800000 | tf_op jit(solution)/shard_map/qkv/pallas_call | solution.py:49
  36.0 7.7 %attend.3 = (bf16[768,384]{1,0:T(8,128)(2,1)S(1)}, bf16[768,256]{1,0:T(8,128)(2,1)S(1)}, bf16[1536,128]{1,0:T(8,128)(2,1)S(1)}, bf16[1536,128]{1,0:T(8,128)(2,1)S(1)}) custom-call(bf16[1536,384]{1,0:T(8,128)(2,1)S(1)} %get-tuple-element.94.q_ref.refs_2_, bf16[1536,384]{1,0:T(8,128)(2,1)S(1)} %get-tuple-element.95.k_ref.refs_3_, ...), custom_call_target="tpu_custom_call" | custom-call | flops 1449551488 | bytes 450000 | tf_op jit(solution)/shard_map/attend/pallas_call | solution.py:289
  47.0 7.7 %attend.4 = (bf16[768,384]{1,0:T(8,128)(2,1)S(1)}, bf16[768,256]{1,0:T(8,128)(2,1)S(1)}, bf16[1536,128]{1,0:T(8,128)(2,1)S(1)}, bf16[1536,128]{1,0:T(8,128)(2,1)S(1)}) custom-call(bf16[1536,384]{1,0:T(8,128)(2,1)S(1)} %get-tuple-element.94.q_ref.refs_2_, ...), custom_call_target="tpu_custom_call", output_to_operand_aliasing={{0}: (5, {}), {1}: (6, {})} | custom-call | flops 1449551488 | bytes 450000 | tf_op jit(solution)/shard_map/attend/pallas_call | solution.py:289
  66.9 8.8 %attend.5 = (bf16[768,384]{1,0:T(8,128)(2,1)S(1)}, bf16[768,128]{1,0:T(8,128)(2,1)}, bf16[1536,128]{1,0:T(8,128)(2,1)S(1)}, bf16[1536,128]{1,0:T(8,128)(2,1)S(1)}) custom-call(bf16[1536,384]{1,0:T(8,128)(2,1)S(1)} %copy-done.19, bf16[1536,384]{1,0:T(8,128)(2,1)S(1)} %copy-done.21, bf16[1536,384]{1,0:T(8,128)(2,1)S(1)} %copy-done.23, ...), custom_call_target="tpu_custom_call", output_to_operand_aliasing={{0}: (5, {})} | custom-call | flops 1449551488 | bytes 450000 | tf_op jit(solution)/shard_map/attend/pallas_call | solution.py:289
  86.1 20.8 %mlp.1 = (bf16[768,768]{1,0:T(8,128)(2,1)}, bf16[768,768]{1,0:T(8,128)(2,1)S(1)}, bf16[768,768]{1,0:T(8,128)(2,1)S(1)}, f32[768,768]{1,0:T(8,128)S(1)}, bf16[768...) custom-call(s32[2]{0:T(128)S(1)} %pad_add_fusion.refs_0_, ...), custom_call_target="tpu_custom_call" | custom-call | flops 2989699840 | bytes 3600000 | tf_op jit(solution)/shard_map/mlp/pallas_call | solution.py:49
  107.3 4.9 %weight_grads.2 = (bf16[1056,768]{1,0:T(8,128)(2,1)S(1)}, bf16[1056,768]{1,0:T(8,128)(2,1)S(1)}) custom-call(s32[1]{0:T(128)} %bitcast.8.refs_0_, bf16[768,256]{1,0:T(8,128)(2,1)} %collective-permute-done.1.refs_9_.refs_4_.refs_1_, bf16[768,128]{1,0:T(8,128)(2,1)} %collective-permute-done.2.refs_5_.refs_2_, ...), custom_call_target="tpu_custom_call" | custom-call | flops 747424960 | bytes 1350000 | tf_op jit(solution)/shard_map/weight_grads/pallas_call | solution.py:49
  112.2 5.4 %collective-permute-done.11.refs_7_.refs_9_ = bf16[768,256]{1,0:T(8,128)(2,1)S(1)} collective-permute-done((bf16[768,256]{1,0:T(8,128)(2,1)S(1)}, bf16[768,256]{1,0:T(8,128)(2,1)S(1)}, u32[]{:S(2)}, u32[]{:S(2)}) %collective-permute-start.11) | collective-permute-done | bytes 393248 | tf_op jit(solution)/shard_map/ppermute | solution.py:733
  117.6 3.1 %weight_grads.3 = (bf16[1056,768]{1,0:T(8,128)(2,1)S(1)}, bf16[1056,768]{1,0:T(8,128)(2,1)S(1)}) custom-call(s32[1]{0:T(128)} %bitcast.8.refs_0_, bf16[768,384]{1,0:T(8,128)(2,1)S(1)} %copy-done.35, bf16[6,768,576]{2,1,0:T(8,128)(2,1)S(1)} %get-tuple-element.115.refs_3_.refs_2_, bf16[768,768]{1,0:T(8,128)(2,1)S(1)} %get-tuple-element.116.refs_4_.refs_3_, ...), custom_call_target="tpu_custom_call" | custom-call | flops 747424960 | bytes 1350000 | tf_op jit(solution)/shard_map/weight_grads/pallas_call | solution.py:49
  121.3 3.1 %collective-permute-done.12.refs_2_ = bf16[1056,768]{1,0:T(8,128)(2,1)S(1)} collective-permute-done((bf16[1056,768]{1,0:T(8,128)(2,1)S(1)}, bf16[1056,768]{1,0:T(8,128)(2,1)S(1)}, u32[]{:S(2)}, u32[]{:S(2)}) %collective-permute-start.12) | collective-permute-done | bytes 1622048 | tf_op jit(solution)/shard_map/ppermute | solution.py:736
  129.9 16.9 %attend_back.3.refs_1_.refs_0_ = bf16[1536,384]{1,0:T(8,128)(2,1)} custom-call(bf16[1536,128]{1,0:T(8,128)(2,1)} %copy-done.61, bf16[1536,128]{1,0:T(8,128)(2,1)} %copy-done.62, bf16[1536,384]{1,0:T(8,128)(2,1)} %copy-done.18, bf16[1536,384]{1,0:T(8,128)(2,1)} %copy-done.20, bf16[1536,384]{1,0:T(8,128)(2,1)} %copy-done.22, bf16[1536,128]{1,0:T(8,128)(2,1)} %copy-done.51, ...), custom_call_target="tpu_custom_call" | custom-call | flops 3623878656 | bytes 900000 | tf_op jit(solution)/shard_map/attend_back/pallas_call | solution.py:49
  161.0 17.3 %attend_back.4.refs_1_ = bf16[1536,384]{1,0:T(8,128)(2,1)} custom-call(bf16[1536,128]{1,0:T(8,128)(2,1)} %copy-done.56, bf16[1536,128]{1,0:T(8,128)(2,1)} %copy-done.57, bf16[1536,384]{1,0:T(8,128)(2,1)} %copy-done.18, bf16[1536,384]{1,0:T(8,128)(2,1)} %copy-done.20, bf16[1536,384]{1,0:T(8,128)(2,1)} %copy-done.22, bf16[1536,128]{1,0:T(8,128)(2,1)} %copy-done.51, ...), custom_call_target="tpu_custom_call" | custom-call | flops 3623878656 | bytes 900000 | tf_op jit(solution)/shard_map/attend_back/pallas_call | solution.py:49
  186.4 17.3 %attend_back.5.refs_2_.refs_1_ = bf16[1536,384]{1,0:T(8,128)(2,1)} custom-call(bf16[1536,128]{1,0:T(8,128)(2,1)} %copy-done.58, bf16[1536,128]{1,0:T(8,128)(2,1)} %copy-done.59, bf16[1536,384]{1,0:T(8,128)(2,1)} %copy-done.18, bf16[1536,384]{1,0:T(8,128)(2,1)} %copy-done.20, bf16[1536,384]{1,0:T(8,128)(2,1)} %copy-done.22, bf16[1536,128]{1,0:T(8,128)(2,1)} %copy-done.51, ...), custom_call_target="tpu_custom_call" | custom-call | flops 3623878656 | bytes 900000 | tf_op jit(solution)/shard_map/attend_back/pallas_call | solution.py:49
  206.7 3.4 %tail.2 = (bf16[768,768]{1,0:T(8,128)(2,1)S(1)}, f32[8,768]{1,0:T(8,128)S(1)}) custom-call(bf16[1536,384]{1,0:T(8,128)(2,1)S(1)} %copy-done.5, bf16[1536,384]{1,0:T(8,128)(2,1)S(1)} %copy-done.6, bf16[1536,384]{1,0:T(8,128)(2,1)S(1)} %copy-done.3, bf16[1152,768]{1,0:T(8,128)(2,1)S(1)} %copy-done.8, bf16[768,768]{1,0:T(8,128)(2,1)} %collective-permute-done.refs_0_.refs_4_, ...), custom_call_target="tpu_custom_call" | custom-call | flops 407686336 | bytes 1200000 | tf_op jit(solution)/shard_map/tail/pallas_call | solution.py:49
  229.6 6.3 %collective-permute-done.26 = f32[2,768]{1,0:T(2,128)S(1)} collective-permute-done((f32[2,768]{1,0:T(2,128)S(1)}, f32[2,768]{1,0:T(2,128)S(1)}, u32[]{:S(2)}, u32[]{:S(2)}) %collective-permute-start.26) | collective-permute-done | bytes 6176 | tf_op jit(solution)/shard_map/ppermute | solution.py:736
  237.7 8.4 %collective-permute-done.33 = bf16[264,768]{1,0:T(8,128)(2,1)S(1)} collective-permute-done((bf16[264,768]{1,0:T(8,128)(2,1)S(1)}, bf16[264,768]{1,0:T(8,128)(2,1)S(1)}, u32[]{:S(2)}, u32[]{:S(2)}) %collective-permute-start.33) | collective-permute-done | bytes 405536 | tf_op jit(solution)/shard_map/ppermute | solution.py:736
  246.3 4.8 %collective-permute-done.27 = bf16[152,768]{1,0:T(8,128)(2,1)S(1)} collective-permute-done((bf16[152,768]{1,0:T(8,128)(2,1)S(1)}, bf16[152,768]{1,0:T(8,128)(2,1)S(1)}, u32[]{:S(2)}, u32[]{:S(2)}) %collective-permute-start.27) | collective-permute-done | bytes 233504 | tf_op jit(solution)/shard_map/ppermute | solution.py:736
  252.0 10.5 %collective-permute-done.34 = bf16[264,768]{1,0:T(8,128)(2,1)S(1)} collective-permute-done((bf16[264,768]{1,0:T(8,128)(2,1)S(1)}, bf16[264,768]{1,0:T(8,128)(2,1)S(1)}, u32[]{:S(2)}, u32[]{:S(2)}) %collective-permute-start.34) | collective-permute-done | bytes 405536 | tf_op jit(solution)/shard_map/ppermute | solution.py:736
  265.9 7.3 %collective-permute-done.29 = bf16[152,768]{1,0:T(8,128)(2,1)S(1)} collective-permute-done((bf16[152,768]{1,0:T(8,128)(2,1)S(1)}, bf16[152,768]{1,0:T(8,128)(2,1)S(1)}, u32[]{:S(2)}, u32[]{:S(2)}) %collective-permute-start.29) | collective-permute-done | bytes 233504 | tf_op jit(solution)/shard_map/ppermute | solution.py:736
  274.9 11.3 %collective-permute-done.35 = bf16[528,768]{1,0:T(8,128)(2,1)S(1)} collective-permute-done((bf16[528,768]{1,0:T(8,128)(2,1)S(1)}, bf16[528,768]{1,0:T(8,128)(2,1)S(1)}, u32[]{:S(2)}, u32[]{:S(2)}) %collective-permute-start.35) | collective-permute-done | bytes 811040 | tf_op jit(solution)/shard_map/ppermute | solution.py:736
  286.6 8.1 %collective-permute-done.31 = bf16[288,768]{1,0:T(8,128)(2,1)S(1)} collective-permute-done((bf16[288,768]{1,0:T(8,128)(2,1)S(1)}, bf16[288,768]{1,0:T(8,128)(2,1)S(1)}, u32[]{:S(2)}, u32[]{:S(2)}) %collective-permute-start.31) | collective-permute-done | bytes 442400 | tf_op jit(solution)/shard_map/ppermute | solution.py:736
  301.5 3.1 %unstack.1 = (f32[384,768]{1,0:T(8,128)}, f32[2,576,768]{2,1,0:T(8,128)}, f32[576,768]{1,0:T(8,128)}) custom-call(s32[1]{0:T(128)} %bitcast.8.refs_0_, bf16[1056,768]{1,0:T(8,128)(2,1)S(1)} %pad_maximum_fusion.refs_1_, bf16[1056,768]{1,0:T(8,128)(2,1)S(1)} %collective-permute-done.36.refs_2_), custom_call_target="tpu_custom_call" | custom-call | flops 15000000 | bytes 1500000 | tf_op jit(solution)/shard_map/unstack/pallas_call | solution.py:49
  (258 shorter events, 107.0 us)
Async XLA Ops:
  0.6 29.3 %collective-permute-start = (bf16[768,768]{1,0:T(8,128)(2,1)}, bf16[768,768]{1,0:T(8,128)(2,1)}, u32[]{:S(2)}, u32[]{:S(2)}) collective-permute-start(bf16[768,768]{1,0:T(8,128)(2,1)} %refs_0_.5), channel_id=1, source_target_pairs={{0,1},{1,0},{2,3},{3,2},{4,5},{5,4},{6,7},{7,6},{8,9},{9,8},{10,11... | collective-permute-start | bytes 3538952 | tf_op jit(solution)/shard_map/ppermute | solution.py:733
  30.0 15.2 %collective-permute-start.3 = (bf16[272,768]{1,0:T(8,128)(2,1)S(1)}, bf16[272,768]{1,0:T(8,128)(2,1)}, u32[]{:S(2)}, u32[]{:S(2)}) collective-permute-start(bf16[272,768]{1,0:T(8,128)(2,1)S(1)} %slice.66), channel_id=1, source_target_pairs={{0,1},{1,0},{2,3},{3,2},{4,5},{5,4},{6,7},{7,6},{8,9},{9,8},{10,11... | collective-permute-start | bytes 1253384 | tf_op jit(solution)/shard_map/ppermute | solution.py:733
  31.8 25.9 %collective-permute-start.7 = (bf16[256,768]{1,0:T(8,128)(2,1)S(1)}, bf16[256,768]{1,0:T(8,128)(2,1)}, u32[]{:S(2)}, u32[]{:S(2)}) collective-permute-start(bf16[256,768]{1,0:T(8,128)(2,1)S(1)} %slice.67), channel_id=1, source_target_pairs={{0,1},{1,0},{2,3},{3,2},{4,5},{5,4},{6,7},{7,6},{8,9},{9,8},{10,11... | collective-permute-start | bytes 1179656 | tf_op jit(solution)/shard_map/ppermute | solution.py:733
  45.2 14.8 %collective-permute-start.4 = (bf16[272,768]{1,0:T(8,128)(2,1)}, bf16[272,768]{1,0:T(8,128)(2,1)}, u32[]{:S(2)}, u32[]{:S(2)}) collective-permute-start(bf16[272,768]{1,0:T(8,128)(2,1)} %collective-permute-done.3.refs_1_), channel_id=1, source_target_pairs={{0,4},{2,6},{4,0},{6,2},{8,12},{10,14},{12,8},{14,10},{16,20},{18,... | collective-permute-start | bytes 1253384 | tf_op jit(solution)/shard_map/ppermute | solution.py:736
  57.7 20.3 %collective-permute-start.8 = (bf16[256,768]{1,0:T(8,128)(2,1)}, bf16[256,768]{1,0:T(8,128)(2,1)}, u32[]{:S(2)}, u32[]{:S(2)}) collective-permute-start(bf16[256,768]{1,0:T(8,128)(2,1)} %collective-permute-done.7.refs_5_), channel_id=1, source_target_pairs={{0,4},{2,6},{4,0},{6,2},{8,12},{10,14},{12,8},{14,10},{16,20},{18,... | collective-permute-start | bytes 1179656 | tf_op jit(solution)/shard_map/ppermute | solution.py:736
  58.1 20.5 %collective-permute-start.9 = (bf16[256,768]{1,0:T(8,128)(2,1)}, bf16[256,768]{1,0:T(8,128)(2,1)}, u32[]{:S(2)}, u32[]{:S(2)}) collective-permute-start(bf16[256,768]{1,0:T(8,128)(2,1)} %collective-permute-done.7.refs_5_), channel_id=1, source_target_pairs={{0,2},{2,0},{4,6},{6,4},{8,10},{10,8},{12,14},{14,12},{16,18},{18,... | collective-permute-start | bytes 1179656 | tf_op jit(solution)/shard_map/ppermute | solution.py:736
  58.1 22.4 %collective-permute-start.1 = (bf16[768,256]{1,0:T(8,128)(2,1)}, bf16[768,256]{1,0:T(8,128)(2,1)}, u32[]{:S(2)}, u32[]{:S(2)}) collective-permute-start(bf16[768,256]{1,0:T(8,128)(2,1)} %copy-done.47), channel_id=1, source_target_pairs={{0,1},{1,0},{2,3},{3,2},{4,5},{5,4},{6,7},{7,6},{8,9},{9,8},{10,11... | collective-permute-start | bytes 1179656 | tf_op jit(solution)/shard_map/ppermute | solution.py:733
  59.9 20.6 %collective-permute-start.5 = (bf16[272,768]{1,0:T(8,128)(2,1)}, bf16[272,768]{1,0:T(8,128)(2,1)}, u32[]{:S(2)}, u32[]{:S(2)}) collective-permute-start(bf16[272,768]{1,0:T(8,128)(2,1)} %collective-permute-done.3.refs_1_), channel_id=1, source_target_pairs={{0,2},{2,0},{4,6},{6,4},{8,10},{10,8},{12,14},{14,12},{16,18},{18,... | collective-permute-start | bytes 1253384 | tf_op jit(solution)/shard_map/ppermute | solution.py:736
  127.8 20.1 %collective-permute-start.14 = (bf16[512,768]{1,0:T(8,128)(2,1)}, bf16[512,768]{1,0:T(8,128)(2,1)}, u32[]{:S(2)}, u32[]{:S(2)}) collective-permute-start(bf16[512,768]{1,0:T(8,128)(2,1)} %get-tuple-element.125.refs_13_), channel_id=1, source_target_pairs={{0,1},{1,0},{2,3},{3,2},{4,5},{5,4},{6,7},{7,6},{8,9},{9,8},{10,11... | collective-permute-start | bytes 2359304 | tf_op jit(solution)/shard_map/ppermute | solution.py:733
  128.1 21.2 %collective-permute-start.15 = (bf16[2,272,768]{2,1,0:T(8,128)(2,1)}, bf16[2,272,768]{2,1,0:T(8,128)(2,1)}, u32[]{:S(2)}, u32[]{:S(2)}) collective-permute-start(bf16[2,272,768]{2,1,0:T(8,128)(2,1)} %get-tuple-element.132), channel_id=1, source_target_pairs={{0,4},{2,6},{4,0},{6,2},{8,12},{10,14},{12,8},{14,10},{16,20},{18,... | collective-permute-start | bytes 2506760 | tf_op jit(solution)/shard_map/ppermute | solution.py:736
  152.4 25.9 %collective-permute-start.18 = (bf16[272,768]{1,0:T(8,128)(2,1)}, bf16[272,768]{1,0:T(8,128)(2,1)}, u32[]{:S(2)}, u32[]{:S(2)}) collective-permute-start(bf16[272,768]{1,0:T(8,128)(2,1)} %slice_bitcast_fusion.1), channel_id=1, source_target_pairs={{0,1},{1,0},{2,3},{3,2},{4,5},{5,4},{6,7},{7,6},{8,9},{9,8},{10,11... | collective-permute-start | bytes 1253384 | tf_op jit(solution)/shard_map/ppermute | solution.py:733
  154.9 23.5 %collective-permute-start.17 = (bf16[256,768]{1,0:T(8,128)(2,1)}, bf16[256,768]{1,0:T(8,128)(2,1)}, u32[]{:S(2)}, u32[]{:S(2)}) collective-permute-start(bf16[256,768]{1,0:T(8,128)(2,1)} %get-tuple-element.168), channel_id=1, source_target_pairs={{0,4},{2,6},{4,0},{6,2},{8,12},{10,14},{12,8},{14,10},{16,20},{18,... | collective-permute-start | bytes 1179656 | tf_op jit(solution)/shard_map/ppermute | solution.py:736
  156.4 30.0 %collective-permute-start.16 = (bf16[768,128]{1,0:T(8,128)(2,1)}, bf16[768,128]{1,0:T(8,128)(2,1)}, u32[]{:S(2)}, u32[]{:S(2)}) collective-permute-start(bf16[768,128]{1,0:T(8,128)(2,1)} %copy-done.48), channel_id=1, source_target_pairs={{0,1},{1,0},{2,3},{3,2},{4,5},{5,4},{6,7},{7,6},{8,9},{9,8},{10,11... | collective-permute-start | bytes 589832 | tf_op jit(solution)/shard_map/ppermute | solution.py:733
  161.0 22.3 %collective-permute-start.21 = (bf16[192,768]{1,0:T(8,128)(2,1)S(1)}, bf16[192,768]{1,0:T(8,128)(2,1)S(1)}, u32[]{:S(2)}, u32[]{:S(2)}) collective-permute-start(bf16[192,768]{1,0:T(8,128)(2,1)S(1)} %get-tuple-element.146), channel_id=1, source_target_pairs={{0,2},{2,0},{4,6},{6,4},{8,10},{10,8},{12,14},{14,12},{16,18},{18,... | collective-permute-start | bytes 884744 | tf_op jit(solution)/shard_map/ppermute | solution.py:736
  181.8 21.9 %collective-permute-start.19 = (bf16[264,768]{1,0:T(8,128)(2,1)}, bf16[264,768]{1,0:T(8,128)(2,1)}, u32[]{:S(2)}, u32[]{:S(2)}) collective-permute-start(bf16[264,768]{1,0:T(8,128)(2,1)} %get-tuple-element.166), channel_id=1, source_target_pairs={{0,8},{2,10},{4,12},{6,14},{8,0},{10,2},{12,4},{14,6},{16,24},{18,... | collective-permute-start | bytes 1216520 | tf_op jit(solution)/shard_map/ppermute | solution.py:736
  186.2 26.9 %collective-permute-start.22 = (bf16[192,768]{1,0:T(8,128)(2,1)S(1)}, bf16[192,768]{1,0:T(8,128)(2,1)}, u32[]{:S(2)}, u32[]{:S(2)}) collective-permute-start(bf16[192,768]{1,0:T(8,128)(2,1)S(1)} %get-tuple-element.147), channel_id=1, source_target_pairs={{0,2},{2,0},{4,6},{6,4},{8,10},{10,8},{12,14},{14,12},{16,18},{18,... | collective-permute-start | bytes 884744 | tf_op jit(solution)/shard_map/ppermute | solution.py:736
  225.5 20.6 %collective-permute-start.33 = (bf16[264,768]{1,0:T(8,128)(2,1)S(1)}, bf16[264,768]{1,0:T(8,128)(2,1)S(1)}, u32[]{:S(2)}, u32[]{:S(2)}) collective-permute-start(bf16[264,768]{1,0:T(8,128)(2,1)S(1)} %copy-done.10), channel_id=1, source_target_pairs={{0,16},{2,18},{4,20},{6,22},{8,24},{10,26},{12,28},{14,30},{16,0},... | collective-permute-start | bytes 1216520 | tf_op jit(solution)/shard_map/ppermute | solution.py:736
  228.1 34.5 %collective-permute-start.20 = (bf16[768,768]{1,0:T(8,128)(2,1)}, bf16[768,768]{1,0:T(8,128)(2,1)S(1)}, u32[]{:S(2)}, u32[]{:S(2)}) collective-permute-start(bf16[768,768]{1,0:T(8,128)(2,1)} %copy-done.25), channel_id=1, source_target_pairs={{0,1},{1,0},{2,3},{3,2},{4,5},{5,4},{6,7},{7,6},{8,9},{9,8},{10,11... | collective-permute-start | bytes 3538952 | tf_op jit(solution)/shard_map/ppermute | solution.py:733
  237.2 13.9 %collective-permute-start.27 = (bf16[152,768]{1,0:T(8,128)(2,1)S(1)}, bf16[152,768]{1,0:T(8,128)(2,1)S(1)}, u32[]{:S(2)}, u32[]{:S(2)}) collective-permute-start(bf16[152,768]{1,0:T(8,128)(2,1)S(1)} %broadcast_select_fusion.15), channel_id=1, source_target_pairs={{0,8},{2,10},{4,12},{6,14},{8,0},{10,2},{12,4},{14,6},{16,24},{18,... | collective-permute-start | bytes 700424 | tf_op jit(solution)/shard_map/ppermute | solution.py:736
  246.3 16.2 %collective-permute-start.34 = (bf16[264,768]{1,0:T(8,128)(2,1)S(1)}, bf16[264,768]{1,0:T(8,128)(2,1)S(1)}, u32[]{:S(2)}, u32[]{:S(2)}) collective-permute-start(bf16[264,768]{1,0:T(8,128)(2,1)S(1)} %add_convert_fusion.3), channel_id=1, source_target_pairs={{0,8},{2,10},{4,12},{6,14},{8,0},{10,2},{12,4},{14,6},{16,24},{18,... | collective-permute-start | bytes 1216520 | tf_op jit(solution)/shard_map/ppermute | solution.py:736
  251.3 14.5 %collective-permute-start.28 = (bf16[152,768]{1,0:T(8,128)(2,1)S(1)}, bf16[152,768]{1,0:T(8,128)(2,1)S(1)}, u32[]{:S(2)}, u32[]{:S(2)}) collective-permute-start(bf16[152,768]{1,0:T(8,128)(2,1)S(1)} %add_convert_fusion.10), channel_id=1, source_target_pairs={{0,16},{2,18},{4,20},{6,22},{8,24},{10,26},{12,28},{14,30},{16,0},... | collective-permute-start | bytes 700424 | tf_op jit(solution)/shard_map/ppermute | solution.py:736
  265.2 20.9 %collective-permute-start.35 = (bf16[528,768]{1,0:T(8,128)(2,1)S(1)}, bf16[528,768]{1,0:T(8,128)(2,1)S(1)}, u32[]{:S(2)}, u32[]{:S(2)}) collective-permute-start(bf16[528,768]{1,0:T(8,128)(2,1)S(1)} %pad_maximum_fusion.1), channel_id=1, source_target_pairs={{0,4},{2,6},{4,0},{6,2},{8,12},{10,14},{12,8},{14,10},{16,20},{18,... | collective-permute-start | bytes 2433032 | tf_op jit(solution)/shard_map/ppermute | solution.py:736
  273.3 21.4 %collective-permute-start.31 = (bf16[288,768]{1,0:T(8,128)(2,1)S(1)}, bf16[288,768]{1,0:T(8,128)(2,1)S(1)}, u32[]{:S(2)}, u32[]{:S(2)}) collective-permute-start(bf16[288,768]{1,0:T(8,128)(2,1)S(1)} %pad_maximum_fusion.3), channel_id=1, source_target_pairs={{0,4},{2,6},{4,0},{6,2},{8,12},{10,14},{12,8},{14,10},{16,20},{18,... | collective-permute-start | bytes 1327112 | tf_op jit(solution)/shard_map/ppermute | solution.py:736
  286.5 15.1 %collective-permute-start.36 = (bf16[1056,768]{1,0:T(8,128)(2,1)S(1)}, bf16[1056,768]{1,0:T(8,128)(2,1)S(1)}, u32[]{:S(2)}, u32[]{:S(2)}) collective-permute-start(bf16[1056,768]{1,0:T(8,128)(2,1)S(1)} %pad_maximum_fusion.refs_1_), channel_id=1, source_target_pairs={{0,2},{2,0},{4,6},{6,4},{8,10},{10,8},{12,14},{14,12},{16,18},{18,... | collective-permute-start | bytes 4866056 | tf_op jit(solution)/shard_map/ppermute | solution.py:736
  (81 other events, 503.1 us)
where the time goes:
time: 309 us; the launch traced here: 305 us
  Pallas kernels  137 us (44%)
  waiting for transfers between devices  81.6 us (26%)
  local copies, waits for them, and re-layouts  35.5 us (11%)
  starting transfers between devices  30.3 us (10%)
  other arithmetic  18.6 us (6%)
    pallas_call x19, Pallas kernels, call(): pl.pallas_call(run, in_specs=list(in_specs) + [pl.BlockSpec(memory_space=...  111 us
    ppermute x26, waiting for transfers between devices, over(): return lax.ppermute(x, 'dp', [(n, n ^ bit) for n in range(dp)])  60.1 us
    unnamed x136, local copies, waits for them, and re-layouts  32.6 us
    pallas_call x3, Pallas kernels, attend(): pl.pallas_call(attend_body, grid=(2,), in_specs=[pl.BlockSpec((rows, PAIR...  24.1 us
    ppermute x11, waiting for transfers between devices, over_y(): return lax.ppermute(x, 'tensor', [(0, 1), (1, 0)])  21.5 us
    ppermute x26, starting transfers between devices, over(): return lax.ppermute(x, 'dp', [(n, n ^ bit) for n in range(dp)])  17.3 us
    ppermute x11, starting transfers between devices, over_y(): return lax.ppermute(x, 'tensor', [(0, 1), (1, 0)])  13 us
    convert_element_type x12, other arithmetic, add(): return (a.astype(f32) + b.astype(f32)).astype(bf16)  11.4 us
  transfers between devices with their start and end apart: 37, of which 14 were waited for; matrix products, arithmetic and copies ran while one was open for 6% of the time, Pallas kernels for 37%

commit v1 on v0

--- a/solution.py
+++ b/solution.py
@@ -311,9 +311,13 @@
 
 
 def back_body(
-    qa_ref, qb_ref, q_ref, k_ref, v_ref, fk_ref, o0_ref, o1_ref, d0_ref, d1_ref, cos_ref, sin_ref,
-    out_ref, dol_ref, da_ref, db_ref, dqt_ref,
+    start, begun, ends, qa_ref, qb_ref, q_ref, k_ref, v_ref, fk_ref, o0_ref, o1_ref, d0_ref, d1_ref, cos_ref, sin_ref,
+    *refs,
 ):
+    dqt_in, low_in = refs[:2] if begun else (None, None)
+    outs = refs[2:-4] if begun else refs[:-4]
+    dol_ref, da_ref, db_ref, dqt_ref = refs[-4:]
+    out_ref = outs[0]
     step = pl.program_id(0)
     half = d0_ref.shape[0]
     cap = 2 * half
@@ -337,7 +341,11 @@
                     jnp.logical_and(jnp.logical_not(mine), slot == NSEG + part), head_bits, tagged
                 )
             out[...] = tagged.astype(bf16)
-        dqt_ref[...] = jnp.zeros_like(dqt_ref)
+        if begun:
+            dqt_ref[...] = dqt_in[...]
+            out_ref[: start * KBLK, PAIR:] = low_in[...]
+        else:
+            dqt_ref[...] = jnp.zeros_like(dqt_ref)
 
     k, v, fk, q, dol = k_ref[...], v_ref[...], fk_ref[...], q_ref[...], dol_ref[...]
     k_turned = k.T
@@ -355,28 +363,48 @@
         at = head * HD
         dqt_ref[at : at + HD] += nn(k_turned[at : at + HD], ds)
     first = lanes_of(0, k.shape)
-    rows = pl.ds(pl.multiple_of(step * KBLK, KBLK), KBLK)
-    dk = jnp.where(first, dks[0], dks[1])
-    out_ref[rows, PAIR : 2 * PAIR] = turn(dk, cos_ref[rows], sin_ref[rows], True).astype(bf16)
-    out_ref[rows, 2 * PAIR :] = jnp.where(first, dvs[0], dvs[1]).astype(bf16)
-
-    @pl.when(step == cap // KBLK - 1)
+    rows = pl.ds(pl.multiple_of((step + start) * KBLK, KBLK), KBLK)
+    dk = turn(jnp.where(first, dks[0], dks[1]), cos_ref[rows], sin_ref[rows], True).astype(bf16)
+    dv = jnp.where(first, dvs[0], dvs[1]).astype(bf16)
+    if ends:
+        out_ref[rows, PAIR : 2 * PAIR] = dk
+        out_ref[rows, 2 * PAIR :] = dv
+    else:
+        outs[1][:, :PAIR] = dk
+        outs[1][:, PAIR:] = dv
+
+    @pl.when(step == pl.num_programs(0) - 1)
     def _():
-        dq = dqt_ref[...].T * 0.125
-        out_ref[:, :PAIR] = turn(dq, cos_ref[...], sin_ref[...], True).astype(bf16)
-
-
-def attend_back(pair, qa, qb, q, k, v, feat_k, o0, o1, d0, d1, cosine, sine, deps=()):
+        if ends:
+            dq = dqt_ref[...].T * 0.125
+            out_ref[:, :PAIR] = turn(dq, cos_ref[...], sin_ref[...], True).astype(bf16)
+        else:
+            out_ref[...] = dqt_ref[...]
+
+
+def attend_back(
+    pair, start, stop, begun, qa, qb, q, k, v, feat_k, o0, o1, d0, d1, cosine, sine, deps=()
+):
     cap = q.shape[0]
+    ends = stop * KBLK == cap
     full = whole((cap, PAIR))
-    block = pl.BlockSpec((KBLK, PAIR), lambda i: (i, pair))
-    part = pl.BlockSpec((KBLK, PAIR), lambda i: (i, 0))
+    block = pl.BlockSpec((KBLK, PAIR), lambda i: (i + start, pair))
+    part = pl.BlockSpec((KBLK, PAIR), lambda i: (i + start, 0))
     column = lambda n: pl.BlockSpec((cap // 2, PAIR), lambda i: (0, n))
-    return call(
-        back_body,
-        (qa, qb, q, k, v, feat_k, o0, o1, d0, d1, cosine, sine,),
-        deps,
-        grid=(cap // KBLK,),
+    if ends:
+        out_specs = [whole((cap, 3 * PAIR))]
+        out_shape = [jax.ShapeDtypeStruct((cap, 3 * PAIR), bf16)]
+    else:
+        out_specs = [whole((PAIR, cap)), pl.BlockSpec((KBLK, 2 * PAIR), lambda i: (i, 0))]
+        out_shape = [
+            jax.ShapeDtypeStruct((PAIR, cap), f32),
+            jax.ShapeDtypeStruct(((stop - start) * KBLK, 2 * PAIR), bf16),
+        ]
+    return call(
+        functools.partial(back_body, start, bool(begun), ends),
+        (qa, qb, q, k, v, feat_k, o0, o1, d0, d1, cosine, sine, *begun),
+        deps,
+        grid=(stop - start,),
         in_specs=[
             full,
             full,
@@ -390,9 +418,10 @@
             column(pair % 2),
             full,
             full,
-        ],
-        out_specs=whole((cap, 3 * PAIR)),
-        out_shape=jax.ShapeDtypeStruct((cap, 3 * PAIR), bf16),
+        ]
+        + [whole(x.shape) for x in begun],
+        out_specs=out_specs,
+        out_shape=out_shape,
         scratch_shapes=[
             pltpu.VMEM((cap, PAIR), bf16),
             pltpu.VMEM((cap, PAIR), bf16),
@@ -400,7 +429,7 @@
             pltpu.VMEM((PAIR, cap), f32),
         ],
         compiler_params=params(58),
-        cost_estimate=cost(5 * 2 * 2 * cap * cap * 256 * 2, 6e6),
+        cost_estimate=cost(5 * 2 * 2 * (stop - start) * KBLK * cap * 256 * 2, 6e6),
         name="attend_back",
     )
 
@@ -535,7 +564,7 @@
         out_shape=[shape] * 2,
         scratch_shapes=[pltpu.VMEM((total, d), bf16), pltpu.SemaphoreType.DMA((2,))],
         compiler_params=params(18),
-        cost_estimate=cost(2 * 2 * rows * d * total, 9e6),
+        cost_estimate=cost(1e5, 1e4),
         name="weight_grads",
     )
 
@@ -554,20 +583,41 @@
 
 def pair_grads(core, back, n1, deps=()):
     cap, d = n1.shape
-    shape = jax.ShapeDtypeStruct((3 * PAIR // 2, d), bf16)
+    rows = back.shape[1]
+    shape = jax.ShapeDtypeStruct((rows // 2, d), bf16)
     vmem = pl.BlockSpec(memory_space=pltpu.VMEM)
     anywhere = pl.BlockSpec(memory_space=pl.ANY)
     return call(
         pair_body,
-        (core, back, n1,),
+        (core, back, n1),
         deps,
         in_specs=[pl.BlockSpec(memory_space=pltpu.SMEM)] + [vmem] * 2,
         out_specs=[anywhere] * 2,
         out_shape=[shape] * 2,
-        scratch_shapes=[pltpu.VMEM((3 * PAIR, d), bf16), pltpu.SemaphoreType.DMA((2,))],
+        scratch_shapes=[pltpu.VMEM((rows, d), bf16), pltpu.SemaphoreType.DMA((2,))],
         compiler_params=params(10),
-        cost_estimate=cost(2 * 2 * cap * d * 3 * PAIR, 5e6),
+        cost_estimate=cost(1e5, 1e4),
         name="pair_grads",
+    )
+
+
+def gains_body(own_ref, other_ref, mlp_ref, out_ref):
+    a = jnp.sum(own_ref[...] + other_ref[...], axis=0, keepdims=True)
+    m = jnp.sum(mlp_ref[...], axis=0, keepdims=True)
+    line = lax.broadcasted_iota(jnp.int32, out_ref.shape, 0)
+    out_ref[...] = jnp.where(line == 0, a, jnp.where(line == 1, m, 0.0))
+
+
+def gain_rows(own, other, mlp_part):
+    vmem = pl.BlockSpec(memory_space=pltpu.VMEM)
+    return call(
+        gains_body,
+        (own, other, mlp_part),
+        in_specs=[vmem] * 3,
+        out_shape=jax.ShapeDtypeStruct(own.shape, f32),
+        compiler_params=params(8),
+        cost_estimate=cost(1e5, 1e4),
+        name="gain_rows",
     )
 
 
@@ -652,8 +702,121 @@
         in_specs=[pl.BlockSpec(memory_space=pltpu.SMEM)] + [vmem] * 4,
         out_shape=[jax.ShapeDtypeStruct((head, d), bf16)] * 2 + [cut] * 2,
         compiler_params=params(20),
-        cost_estimate=cost(4 * rows * d, 12e6),
+        cost_estimate=cost(1e5, 1e4),
         name="combine",
+    )
+
+
+def second_body(side_ref, own_ref, got_a, mine_ref, got_b, keep_ref, pair_ref, far_ref, over_ref):
+    low = side_ref[0] == 0
+    total = (own_ref[...].astype(f32) + got_a[...].astype(f32)).astype(bf16)
+    half = total.shape[0] // 2
+    first, second = total[:half], total[half:]
+    keep_ref[...] = jnp.where(low, first, second)
+    over_ref[...] = jnp.where(low, second, first)
+    pair = (mine_ref[...].astype(f32) + got_b[...].astype(f32)).astype(bf16)
+    pair_ref[...] = pair[0]
+    far_ref[...] = pair[1]
+
+
+def second_step(side, own, got_a, mine, got_b, deps=()):
+    rows, d = own.shape
+    half = mine.shape[1]
+    vmem = pl.BlockSpec(memory_space=pltpu.VMEM)
+    return call(
+        second_body,
+        (side, own, got_a, mine, got_b),
+        deps,
+        in_specs=[pl.BlockSpec(memory_space=pltpu.SMEM)] + [vmem] * 4,
+        out_shape=[
+            jax.ShapeDtypeStruct((rows // 2, d), bf16),
+            jax.ShapeDtypeStruct((half, d), bf16),
+            jax.ShapeDtypeStruct((half, d), bf16),
+            jax.ShapeDtypeStruct((rows // 2, d), bf16),
+        ],
+        compiler_params=params(14),
+        cost_estimate=cost(1e5, 1e4),
+        name="second_step",
+    )
+
+
+def cut_body(low_ref, *refs):
+    *terms, keep_ref, over_ref = refs
+    low = low_ref[0] == 0
+    sums = [
+        terms[n][...].astype(f32) + terms[n + 1][...].astype(f32) for n in range(0, len(terms), 2)
+    ]
+    short = 2 * keep_ref.shape[0] - sum(x.shape[0] for x in sums)
+    if short:
+        sums.append(jnp.zeros((short, sums[0].shape[1]), f32))
+    total = jnp.concatenate(sums, axis=0)
+    half = total.shape[0] // 2
+    first, second = total[:half], total[half:]
+    keep_ref[...] = jnp.where(low, first, second).astype(bf16)
+    over_ref[...] = jnp.where(low, second, first).astype(bf16)
+
+
+def cut_sums(low, terms, deps=()):
+    rows = (sum(x.shape[0] for x in terms) // 2 + 31) // 32 * 32
+    vmem = pl.BlockSpec(memory_space=pltpu.VMEM)
+    return call(
+        cut_body,
+        (low, *terms),
+        deps,
+        in_specs=[pl.BlockSpec(memory_space=pltpu.SMEM)] + [vmem] * len(terms),
+        out_shape=[jax.ShapeDtypeStruct((rows // 2, terms[0].shape[1]), bf16)] * 2,
+        compiler_params=params(12),
+        cost_estimate=cost(1e5, 1e4),
+        name="cut_sums",
+    )
+
+
+def plus_body(a_ref, b_ref, out_ref):
+    out_ref[...] = (a_ref[...].astype(f32) + b_ref[...].astype(f32)).astype(bf16)
+
+
+def plus(a, b, deps=()):
+    vmem = pl.BlockSpec(memory_space=pltpu.VMEM)
+    return call(
+        plus_body,
+        (a, b),
+        deps,
+        in_specs=[vmem] * 2,
+        out_shape=jax.ShapeDtypeStruct(a.shape, bf16),
+        compiler_params=params(8),
+        cost_estimate=cost(1e5, 1e4),
+        name="plus",
+    )
+
+
+def pairs_body(side_ref, first_ref, keep, came, mine_ref, other_ref):
+    low = side_ref[0] == 0
+    first = first_ref[...]
+    second = (keep[...].astype(f32) + came[...].astype(f32)).astype(bf16)
+    mine_ref[...] = jnp.where(low, first, second)
+    other_ref[...] = jnp.where(low, second, first)
+
+
+def last_pair_body(side_ref, keep, came, mine_ref, other_ref):
+    low = side_ref[0] == 0
+    total = (keep[...].astype(f32) + came[...].astype(f32)).astype(bf16)
+    half = total.shape[0] // 2
+    mine_ref[...] = jnp.where(low, total[:half], total[half:])
+    other_ref[...] = jnp.where(low, total[half:], total[:half])
+
+
+def pairs_step(side, arrays, rows, deps=()):
+    vmem = pl.BlockSpec(memory_space=pltpu.VMEM)
+    shape = jax.ShapeDtypeStruct((rows, arrays[0].shape[1]), bf16)
+    return call(
+        pairs_body if len(arrays) == 3 else last_pair_body,
+        (side, *arrays),
+        deps,
+        in_specs=[pl.BlockSpec(memory_space=pltpu.SMEM)] + [vmem] * len(arrays),
+        out_shape=[shape] * 2,
+        compiler_params=params(10),
+        cost_estimate=cost(1e5, 1e4),
+        name="pairs_step",
     )
 
 
@@ -688,26 +851,28 @@
             jax.ShapeDtypeStruct((8, d), f32),
         ],
         compiler_params=params(14),
-        cost_estimate=cost(2 * 2 * rows * w.size, 8e6),
+        cost_estimate=cost(1e5, 1e4),
         name="tail",
     )
 
 
-def last_body(h_ref, gain_ref, own_ref, got_ref, dx_ref, out_ref):
+def last_body(h_ref, gain_ref, own_ref, got_ref, late_ref, dx_ref, out_ref):
     xh, inv = unit_rows(h_ref[...].astype(f32))
-    dn = own_ref[...] + got_ref[...].astype(f32)
+    got = jnp.where(pl.program_id(0) == 0, got_ref[...].astype(f32), late_ref[...].astype(f32))
+    dn = own_ref[...] + got
     out_ref[...] = (dx_ref[...] + norm_back(dn * gain_ref[...], xh, inv)).astype(bf16)
 
 
-def last(h, gain, own, got, dx, deps=()):
+def last(h, gain, own, got, late, dx, deps=()):
     rows, d = h.shape
-    row = pl.BlockSpec((BLK, d), lambda i: (i, 0))
+    half = rows // 2
+    row = pl.BlockSpec((half, d), lambda i: (i, 0))
     return call(
         last_body,
-        (h, gain, own, got, dx,),
-        deps,
-        grid=(rows // BLK,),
-        in_specs=[row, whole((1, d)), row, row, row],
+        (h, gain, own, got, late, dx),
+        deps,
+        grid=(2,),
+        in_specs=[row, whole((1, d)), row, whole((half, d)), whole((half, d)), row],
         out_specs=row,
         out_shape=jax.ShapeDtypeStruct((rows, d), bf16),
         compiler_params=params(12),
@@ -787,16 +952,11 @@
     d_got = [over_y(db01), over_y(db2)]
     d_far = (d_got[0], d_got[0], d_got[1])
 
-    def back(pair, *deps):
-        out = attend_back(
-            pair, *q_tag[pair], q, k, v, feat_k, o_own, o_far[pair], d_own, d_far[pair],
-            cosine, sine, deps,
+    def back(pair, start, stop, begun, *deps):
+        return attend_back(
+            pair, start, stop, begun, *q_tag[pair], q, k, v, feat_k, o_own, o_far[pair],
+            d_own, d_far[pair], cosine, sine, deps,
         )
-        return out
-
-    def pair_sum(out, *deps):
-        keep, send = pair_grads(core_at, out, n1, deps)
-        return add(keep, over_core(send))
 
     def split(x, bit):
         low = (place & bit) == 0
@@ -817,71 +977,107 @@
         return merge(mine, bits[2])
 
     keep1, send1 = weight_grads(1, core_at, o_got, by_unit, n2, ga, gm)
-    keep0, send0 = weight_grads(0, core_at, (o_own,), by_unit, n2, ga, gm, (keep1, d_got[0]))
-    came1 = over_core(after(send1, d_got[0]))
-    came0 = over_core(send0)
+    keep0, send0 = weight_grads(0, core_at, (o_own,), by_unit, n2, ga, gm, (keep1,))
+    came1 = over_core(send1)
+    came0 = over_core(after(send0, d_got[0]))
     head = send0.shape[0] // 32 * 16 - 16
     own_a, far_a, mine_b, other_b = combine(
         side.astype(jnp.int32).reshape(1), keep0, came0, keep1, came1, head
     )
     got_a, got_b = over_y(far_a), over(other_b, 2)
-    back0 = back(0, mine_b, far_a)
+    blocks = cap // KBLK
+    back0 = back(0, 0, blocks, (), mine_b, far_a)[0]
     keep, send = pair_grads(core_at, back0, n1)
-    pair0 = add(keep, over_core(send))
-
-    own_a = add(own_a, after(got_a, back0))
-    mine_b = add(mine_b, after(got_b, back0))
-    mine_a, other_a = split(own_a, 2)
-    got_a, got_b = over(other_a, 2), over_y(mine_b[1])
-    back1 = back(1, keep, mine_a, mine_b)
+
+    side_at = side.astype(jnp.int32).reshape(1)
+    mine, mine_b, far_b, other_a = second_step(side_at, own_a, got_a, mine_b, got_b, (back0,))
+    got_a, got_b = over(other_a, 2), over_y(far_b)
+    begun = back(1, 0, 1, (), keep, mine)
+    pair0 = plus(keep, over_core(send))
+
+    if len(bits) > 2:
+        low = ((place // 4) % 2).astype(jnp.int32).reshape(1)
+        mine, other = cut_sums(low, (mine, got_a, mine_b, got_b), (begun[0],))
+        got = over(other, bits[2])
+    else:
+        mine = jnp.concatenate([add(mine, got_a), add(mine_b, got_b)], axis=0)
+    back1 = back(1, 1, blocks, begun, mine, pair0)[0]
     keep, send = pair_grads(core_at, back1, n1)
-    pair1 = add(keep, over_core(send))
-
-    got_a, got_b = after((got_a, got_b), back1)
-    mine = jnp.concatenate([add(mine_a, got_a), add(mine_b[0], got_b)], axis=0)
+
     if len(bits) > 2:
-        mine, other = split(mine, bits[2])
-        got = over(other, bits[2])
-    back2 = back(2, keep, mine)
+        mine = plus(mine, got, (back1,))
+    if len(bits) > 3:
+        got = over(mine, bits[3])
+    came = over_core(send)
+    q_mine, q_other = pairs_step(side_at, (pair0, keep, came), pair0.shape[0])
+    q_got = over(q_other, 2)
+    back2 = back(2, 0, blocks, (), mine, q_other)[0]
+    if len(bits) > 3:
+        mine = plus(mine, got, (back2,))
+    parts = (back0, back1, back2)
+    keep, send = pair_grads(core_at, back2, n1, (mine, q_got))
+    dn_other, gg_other = tail(parts, w_qkv_turned, hidden_got, rows, bf16, (keep,))
+    cut_at = rows // 2
+    dn_got = over_y(dn_other[:cut_at])
+    came = over_core(send)
     if len(bits) > 2:
-        mine = add(mine, after(got, back2))
-    parts = (back0, back1, back2)
-    dn_other, gg_other = tail(parts, w_qkv_turned, hidden_got, rows, bf16, (mine,))
-    dn_got = over_y(dn_other)
-    keep, send = pair_grads(core_at, back2, n1, (dn_other,))
-    pair2 = add(keep, over_core(send))
-    dn_own, gg_own = tail(parts, w_qkv_turned, hidden_in, 0, f32, (keep,))
-
-    if len(bits) > 2:
-        for bit in bits[3:]:
+        for bit in bits[4:]:
             mine = add(mine, over(mine, bit))
         mine = merge(mine, bits[2])
-    grad_in = last(hidden_in, gain_a, dn_own, dn_got, dx)
-    got = over(after(mine, grad_in), 2)
-    low = (place & 2) == 0
-    grads = jnp.concatenate(
-        [in_order(low, mine[: head // 2], got[: head // 2]),
-         in_order(low, mine[head // 2 :], got[head // 2 :])],
-        axis=0,
-    )
-
-    gains = jnp.stack(
-        [jnp.sum(gg_own, axis=0) + jnp.sum(gg_other, axis=0), jnp.sum(gg_mlp, axis=0)]
-    )
+    last_mine, last_other = pairs_step(
+        side_at, (keep, came), pair0.shape[0] // 2, (dn_other,)
+    )
+    dn_own, gg_own = tail(parts, w_qkv_turned, hidden_in, 0, f32, (last_other,))
+    gains = gain_rows(gg_own, gg_other, gg_mlp)
     gains = gains + over_core(gains)
-    gains = gains + over(gains, 2)
-    gains = jnp.pad(gains, ((0, 14), (0, 0))).astype(bf16)
-    mine, other = split(jnp.concatenate([pair0, pair1, pair2], axis=0), 2)
-    mine = add(mine, over(other, 2))
-    count = mine.shape[0]
-    mine = over_rest(jnp.concatenate([mine, gains], axis=0))
+    last_got = over(last_other, 2)
+    weights = mine
+    if len(bits) > 2:
+        mine, other = cut_sums(
+            low, (q_mine, q_got, last_mine, last_got, gains, over(gains, 2)), (dn_got,)
+        )
+        lent = over(other, bits[2])
+        got = over(after(weights, mine), 2)
+        low_side = (place & 2) == 0
+        grads = jnp.concatenate(
+            [in_order(low_side, weights[: head // 2], got[: head // 2]),
+             in_order(low_side, weights[head // 2 : quarter], got[head // 2 : quarter])],
+            axis=0,
+        )
+        mine = plus(mine, lent)
+        dn_late = over_y(after(dn_other[cut_at:], mine))
+        for bit in bits[3:-1]:
+            mine = plus(mine, over(mine, bit))
+        if len(bits) > 3:
+            mine = plus(mine, over(mine, bits[-1]), (got,))
+        mine = merge(mine, bits[2])
+    else:
+        mine = jnp.concatenate(
+            [add(q_mine, q_got), add(last_mine, last_got), add(gains, over(gains, 2))], axis=0
+        )
+        dn_late = over_y(dn_other[cut_at:])
+        got = over(after(weights, mine), 2)
+        low_side = (place & 2) == 0
+        grads = jnp.concatenate(
+            [in_order(low_side, weights[: head // 2], got[: head // 2]),
+             in_order(low_side, weights[head // 2 : quarter], got[head // 2 : quarter])],
+            axis=0,
+        )
+    low_side = (place & 2) == 0
+    grad_in = last(hidden_in, gain_a, dn_own, dn_got, dn_late, dx)
+    first, count = pair0.shape[0], 3 * pair0.shape[0] // 2
     gains = mine[count : count + 2].astype(f32)
     gains = gains + over_y(gains)
-    pairs = merge(mine[:count], 2)
+    got = over(after(mine[:count], grad_in), 2)
+    pairs = jnp.concatenate(
+        [in_order(low_side, mine[:first], got[:first]),
+         in_order(low_side, mine[first:count], got[first:])],
+        axis=0,
+    )
 
     grad_w_attn, grad_w_in, grad_w_out = unstack(core_at, grads, over_core(grads), width, units)
     grad_w_in = jnp.swapaxes(grad_w_in, 1, 2)
-    grad_w_qkv = unpair(core_at, pairs, over_core(pairs))
+    grad_w_qkv = unpair(core_at, pairs, over_core(after(pairs, grad_w_attn)))
     return (
         hidden_out,
         grad_in,

time: 309 us -> 284 us (0.919)
  waiting for transfers between devices: 81.6 us -> 56.5 us
  other arithmetic: 18.6 us -> 3.68 us
  Pallas kernels: 137 us -> 145 us
  starting transfers between devices: 30.3 us -> 36.2 us
    ppermute x26 -> x27, waiting for transfers between devices: 60.1 us -> 30.5 us  [over(): return lax.ppermute(x, 'dp', [(n, n ^ bit) for n in range(dp)])]
    convert_element_type x12 -> x0, other arithmetic: 11.4 us -> none  [add(): return (a.astype(f32) + b.astype(f32)).astype(bf16)]
    pallas_call x19 -> x31, Pallas kernels: 111 us -> 120 us  [call(): pl.pallas_call(run, in_specs=list(in_specs) + [pl.BlockSpec(memory_space=...]
    ppermute x11 -> x12, waiting for transfers between devices: 21.5 us -> 26 us  [over_y(): return lax.ppermute(x, 'tensor', [(0, 1), (1, 0)])]
    ppermute x26 -> x27, starting transfers between devices: 17.3 us -> 21.9 us  [over(): return lax.ppermute(x, 'dp', [(n, n ^ bit) for n in range(dp)])]
    select_n x4 -> x0, other arithmetic: 3.35 us -> none  [split(): return (jnp.where(low, first, second), jnp.where(low, second, first))]
    ppermute x11 -> x12, starting transfers between devices: 13 us -> 14.3 us  [over_y(): return lax.ppermute(x, 'tensor', [(0, 1), (1, 0)])]
    unnamed x136 -> x154, local copies, waits for them, and re-layouts: 32.6 us -> 33.5 us
  transfers between devices with their start and end apart: 37 -> 39, of which waited for: 14 -> 16; matrix products, arithmetic and copies ran while one was open for 6% -> 2% of each run, Pallas kernels for 37% -> 41%
where the time goes in v1:
time: 284 us; the launch traced here: 280 us
  Pallas kernels  145 us (51%)
  waiting for transfers between devices  56.5 us (20%)
  local copies, waits for them, and re-layouts  36.7 us (13%)
  starting transfers between devices  36.2 us (13%)
  other arithmetic  3.68 us (1%)
    pallas_call x31, Pallas kernels, call(): pl.pallas_call(run, in_specs=list(in_specs) + [pl.BlockSpec(memory_space=...  120 us
    unnamed x154, local copies, waits for them, and re-layouts  33.5 us
    ppermute x27, waiting for transfers between devices, over(): return lax.ppermute(x, 'dp', [(n, n ^ bit) for n in range(dp)])  30.5 us
    ppermute x12, waiting for transfers between devices, over_y(): return lax.ppermute(x, 'tensor', [(0, 1), (1, 0)])  26 us
    pallas_call x3, Pallas kernels, attend(): pl.pallas_call(attend_body, grid=(2,), in_specs=[pl.BlockSpec((rows, PAIR...  23.3 us
    ppermute x27, starting transfers between devices, over(): return lax.ppermute(x, 'dp', [(n, n ^ bit) for n in range(dp)])  21.9 us
    ppermute x12, starting transfers between devices, over_y(): return lax.ppermute(x, 'tensor', [(0, 1), (1, 0)])  14.3 us
  transfers between devices with their start and end apart: 39, of which 16 were waited for; matrix products, arithmetic and copies ran while one was open for 2% of the time, Pallas kernels for 41%

profile of v1, /device:TPU:0, one launch (start us, length us, event | category | flops | bytes accessed | tf_op | source)
XLA Modules:
  0.0 280.2 jit_solution(10157841720446246911)
XLA Ops:
  0.6 3.0 %collective-permute-start = (bf16[768,768]{1,0:T(8,128)(2,1)}, bf16[768,768]{1,0:T(8,128)(2,1)}, u32[]{:S(2)}, u32[]{:S(2)}) collective-permute-start(bf16[768,768]{1,0:T(8,128)(2,1)} %refs_0_.5), channel_id=1, source_target_pairs={{0,1},{1,0},{2,3},{3,2},{4,5},{5,4},{6,7},{7,6},{8,9},{9,8},{10,11... | collective-permute-start | bytes 3538952 | tf_op jit(solution)/shard_map/ppermute | solution.py:898
  16.6 2.9 %qkv.2 = (bf16[1536,768]{1,0:T(8,128)(2,1)S(1)}, bf16[1536,384]{1,0:T(8,128)(2,1)S(1)}, bf16[1536,384]{1,0:T(8,128)(2,1)S(1)}, bf16[1536,384]{1,0:T(8,128)(2,1)S(1)}) custom-call(bf16[768,768]{1,0:T(8,128)(2,1)S(1)} %copy-done.16, f32[1,768]{1,0:T(1,128)S(1)} %reshape.43.refs_1_, bf16[3,768,384]{2,1,0:T(8,128)(2,1)S(1)} %copy-done.7, ...), custom_call_target="tpu_custom_call" | custom-call | flops 407686336 | bytes 1800000 | tf_op jit(solution)/shard_map/qkv/pallas_call | solution.py:49
  19.6 10.4 %collective-permute-done.refs_0_.refs_4_ = bf16[768,768]{1,0:T(8,128)(2,1)} collective-permute-done((bf16[768,768]{1,0:T(8,128)(2,1)}, bf16[768,768]{1,0:T(8,128)(2,1)}, u32[]{:S(2)}, u32[]{:S(2)}) %collective-permute-start) | collective-permute-done | bytes 1179680 | tf_op jit(solution)/shard_map/ppermute | solution.py:898
  32.2 3.8 %qkv.3 = (bf16[1536,768]{1,0:T(8,128)(2,1)S(1)}, bf16[1536,384]{1,0:T(8,128)(2,1)S(1)}, bf16[1536,384]{1,0:T(8,128)(2,1)S(1)}, bf16[1536,384]{1,0:T(8,128)(2,1)S(1)}) custom-call(bf16[768,768]{1,0:T(8,128)(2,1)} %collective-permute-done.refs_0_.refs_4_, ...), custom_call_target="tpu_custom_call", output_to_operand_aliasing={{0}: (5, {}), {1}: (6, {}), {2}: (7, {}), {3}: (8, {})} | custom-call | flops 407686336 | bytes 1800000 | tf_op jit(solution)/shard_map/qkv/pallas_call | solution.py:49
  36.0 7.5 %attend.3 = (bf16[768,384]{1,0:T(8,128)(2,1)S(1)}, bf16[768,256]{1,0:T(8,128)(2,1)S(1)}, bf16[1536,128]{1,0:T(8,128)(2,1)S(1)}, bf16[1536,128]{1,0:T(8,128)(2,1)S(1)}) custom-call(bf16[1536,384]{1,0:T(8,128)(2,1)S(1)} %get-tuple-element.106.q_ref.refs_2_, bf16[1536,384]{1,0:T(8,128)(2,1)S(1)} %get-tuple-element.107.k_ref.refs_3_, ...), custom_call_target="tpu_custom_call" | custom-call | flops 1449551488 | bytes 450000 | tf_op jit(solution)/shard_map/attend/pallas_call | solution.py:289
  46.0 7.5 %attend.4 = (bf16[768,384]{1,0:T(8,128)(2,1)S(1)}, bf16[768,256]{1,0:T(8,128)(2,1)S(1)}, bf16[1536,128]{1,0:T(8,128)(2,1)S(1)}, bf16[1536,128]{1,0:T(8,128)(2,1)S(1)}) custom-call(bf16[1536,384]{1,0:T(8,128)(2,1)S(1)} %get-tuple-element.106.q_ref.refs_2_, ...), custom_call_target="tpu_custom_call", output_to_operand_aliasing={{0}: (5, {}), {1}: (6, {})} | custom-call | flops 1449551488 | bytes 450000 | tf_op jit(solution)/shard_map/attend/pallas_call | solution.py:289
  63.3 8.3 %attend.5 = (bf16[768,384]{1,0:T(8,128)(2,1)S(1)}, bf16[768,128]{1,0:T(8,128)(2,1)}, bf16[1536,128]{1,0:T(8,128)(2,1)S(1)}, bf16[1536,128]{1,0:T(8,128)(2,1)S(1)}) custom-call(bf16[1536,384]{1,0:T(8,128)(2,1)S(1)} %copy-done.11, bf16[1536,384]{1,0:T(8,128)(2,1)S(1)} %copy-done.13, bf16[1536,384]{1,0:T(8,128)(2,1)S(1)} %copy-done.15, ...), custom_call_target="tpu_custom_call", output_to_operand_aliasing={{0}: (5, {})} | custom-call | flops 1449551488 | bytes 450000 | tf_op jit(solution)/shard_map/attend/pallas_call | solution.py:289
  76.0 2.8 assemble.1.refs_8_
  78.8 2.8 %collective-permute-done.2.refs_5_.refs_2_ = bf16[768,128]{1,0:T(8,128)(2,1)} collective-permute-done((bf16[768,128]{1,0:T(8,128)(2,1)}, bf16[768,128]{1,0:T(8,128)(2,1)}, u32[]{:S(2)}, u32[]{:S(2)}) %collective-permute-start.2) | collective-permute-done | bytes 196640 | tf_op jit(solution)/shard_map/ppermute | solution.py:898
  81.6 20.3 %mlp.1 = (bf16[768,768]{1,0:T(8,128)(2,1)}, bf16[768,768]{1,0:T(8,128)(2,1)S(1)}, bf16[768,768]{1,0:T(8,128)(2,1)S(1)}, f32[768,768]{1,0:T(8,128)S(1)}, bf16[768...) custom-call(s32[2]{0:T(128)S(1)} %pad_add_fusion.refs_0_, ...), custom_call_target="tpu_custom_call" | custom-call | flops 2989699840 | bytes 3600000 | tf_op jit(solution)/shard_map/mlp/pallas_call | solution.py:49
  102.3 5.1 %weight_grads.2 = (bf16[1056,768]{1,0:T(8,128)(2,1)S(1)}, bf16[1056,768]{1,0:T(8,128)(2,1)S(1)}) custom-call(s32[1]{0:T(128)} %bitcast.8.refs_0_, bf16[768,256]{1,0:T(8,128)(2,1)} %collective-permute-done.1.refs_9_.refs_4_.refs_1_, bf16[768,128]{1,0:T(8,128)(2,1)} %collective-permute-done.2.refs_5_.refs_2_, ...), custom_call_target="tpu_custom_call" | custom-call | flops 15000 | bytes 1500 | tf_op jit(solution)/shard_map/weight_grads/pallas_call | solution.py:49
  107.4 3.1 %weight_grads.3 = (bf16[1056,768]{1,0:T(8,128)(2,1)S(1)}, bf16[1056,768]{1,0:T(8,128)(2,1)S(1)}) custom-call(s32[1]{0:T(128)} %bitcast.8.refs_0_, bf16[768,384]{1,0:T(8,128)(2,1)S(1)} %copy-done.21, bf16[6,768,576]{2,1,0:T(8,128)(2,1)S(1)} %get-tuple-element.127.refs_3_.refs_2_, bf16[768,768]{1,0:T(8,128)(2,1)S(1)} %get-tuple-element.128.refs_4_.refs_3_, ...), custom_call_target="tpu_custom_call" | custom-call | flops 15000 | bytes 1500 | tf_op jit(solution)/shard_map/weight_grads/pallas_call | solution.py:49
  114.1 2.7 collective-permute-done.12.refs_2_
  121.8 16.9 %attend_back.4.refs_1_.refs_5_.refs_0_ = bf16[1536,384]{1,0:T(8,128)(2,1)} custom-call(bf16[1536,128]{1,0:T(8,128)(2,1)} %copy-done.68, bf16[1536,128]{1,0:T(8,128)(2,1)} %copy-done.69, bf16[1536,384]{1,0:T(8,128)(2,1)} %copy-done.10, bf16[1536,384]{1,0:T(8,128)(2,1)} %copy-done.12, bf16[1536,384]{1,0:T(8,128)(2,1)} %copy-done.14, ...), custom_call_target="tpu_custom_call" | custom-call | flops 3623878656 | bytes 900000 | tf_op jit(solution)/shard_map/attend_back/pallas_call | solution.py:49
  152.5 7.4 %attend_back.5 = (f32[128,1536]{1,0:T(8,128)}, bf16[512,256]{1,0:T(8,128)(2,1)}) custom-call(bf16[1536,128]{1,0:T(8,128)(2,1)} %copy-done.36, bf16[1536,128]{1,0:T(8,128)(2,1)} %copy-done.37, bf16[1536,384]{1,0:T(8,128)(2,1)} %copy-done.10, bf16[1536,384]{1,0:T(8,128)(2,1)} %copy-done.12, bf16[1536,384]{1,0:T(8,128)(2,1)} %copy-done.14, ...), custom_call_target="tpu_custom_call" | custom-call | flops 1207959552 | bytes 900000 | tf_op jit(solution)/shard_map/attend_back/pallas_call | solution.py:49
  164.8 13.2 %attend_back.6.refs_2_.refs_1_ = bf16[1536,384]{1,0:T(8,128)(2,1)} custom-call(bf16[1536,128]{1,0:T(8,128)(2,1)} %copy-done.36, bf16[1536,128]{1,0:T(8,128)(2,1)} %copy-done.37, bf16[1536,384]{1,0:T(8,128)(2,1)} %copy-done.10, bf16[1536,384]{1,0:T(8,128)(2,1)} %copy-done.12, bf16[1536,384]{1,0:T(8,128)(2,1)} %copy-done.14, bf16[1536,128]{1,0:T(8,128)(2,1)} %copy-done.35, ...), custom_call_target="tpu_custom_call" | custom-call | flops 2415919104 | bytes 900000 | tf_op jit(solution)/shard_map/attend_back/pallas_call | solution.py:49
  188.6 17.2 %attend_back.7.refs_2_.refs_1_ = bf16[1536,384]{1,0:T(8,128)(2,1)} custom-call(bf16[1536,128]{1,0:T(8,128)(2,1)} %copy-done.66, bf16[1536,128]{1,0:T(8,128)(2,1)} %copy-done.67, bf16[1536,384]{1,0:T(8,128)(2,1)} %copy-done.10, bf16[1536,384]{1,0:T(8,128)(2,1)} %copy-done.12, bf16[1536,384]{1,0:T(8,128)(2,1)} %copy-done.14, bf16[1536,128]{1,0:T(8,128)(2,1)} %copy-done.35, ...), custom_call_target="tpu_custom_call" | custom-call | flops 3623878656 | bytes 900000 | tf_op jit(solution)/shard_map/attend_back/pallas_call | solution.py:49
  211.3 3.4 %tail.2 = (bf16[768,768]{1,0:T(8,128)(2,1)S(1)}, f32[8,768]{1,0:T(8,128)S(1)}) custom-call(bf16[1536,384]{1,0:T(8,128)(2,1)S(1)} %copy-done.3, bf16[1536,384]{1,0:T(8,128)(2,1)S(1)} %copy-done.1, bf16[1536,384]{1,0:T(8,128)(2,1)S(1)} %copy-done.5, bf16[1152,768]{1,0:T(8,128)(2,1)S(1)} %copy-done.19, bf16[768,768]{1,0:T(8,128)(2,1)} %collective-permute-done.refs_0_.refs_4_, ...), custom_call_target="tpu_custom_call" | custom-call | flops 15000 | bytes 1500 | tf_op jit(solution)/shard_map/tail/pallas_call | solution.py:49
  227.7 3.5 %collective-permute-done.25.refs_7_.refs_3_ = bf16[384,768]{1,0:T(8,128)(2,1)S(1)} collective-permute-done((bf16[384,768]{1,0:T(8,128)(2,1)}, bf16[384,768]{1,0:T(8,128)(2,1)S(1)}, u32[]{:S(2)}, u32[]{:S(2)}) %collective-permute-start.25) | collective-permute-done | bytes 589856 | tf_op jit(solution)/shard_map/ppermute | solution.py:898
  234.2 5.5 %collective-permute-done.29.refs_1_ = bf16[160,768]{1,0:T(8,128)(2,1)S(1)} collective-permute-done((bf16[160,768]{1,0:T(8,128)(2,1)S(1)}, bf16[160,768]{1,0:T(8,128)(2,1)S(1)}, u32[]{:S(2)}, u32[]{:S(2)}) %collective-permute-start.29) | collective-permute-done | bytes 245792 | tf_op jit(solution)/shard_map/ppermute | solution.py:901
  243.7 8.4 %collective-permute-done.31.refs_1_ = bf16[160,768]{1,0:T(8,128)(2,1)S(1)} collective-permute-done((bf16[160,768]{1,0:T(8,128)(2,1)S(1)}, bf16[160,768]{1,0:T(8,128)(2,1)S(1)}, u32[]{:S(2)}, u32[]{:S(2)}) %collective-permute-start.31) | collective-permute-done | bytes 245792 | tf_op jit(solution)/shard_map/ppermute | solution.py:901
  256.0 2.7 last.1
  260.0 10.0 %collective-permute-done.36 = bf16[288,768]{1,0:T(8,128)(2,1)S(1)} collective-permute-done((bf16[288,768]{1,0:T(8,128)(2,1)S(1)}, bf16[288,768]{1,0:T(8,128)(2,1)S(1)}, u32[]{:S(2)}, u32[]{:S(2)}) %collective-permute-start.36) | collective-permute-done | bytes 442400 | tf_op jit(solution)/shard_map/ppermute | solution.py:901
  270.2 3.1 %unstack.1 = (f32[384,768]{1,0:T(8,128)}, f32[2,576,768]{2,1,0:T(8,128)}, f32[576,768]{1,0:T(8,128)}) custom-call(s32[1]{0:T(128)} %bitcast.8.refs_0_, bf16[1056,768]{1,0:T(8,128)(2,1)S(1)} %pad_maximum_fusion.refs_1_, bf16[1056,768]{1,0:T(8,128)(2,1)S(1)} %collective-permute-done.37.refs_2_), custom_call_target="tpu_custom_call" | custom-call | flops 15000000 | bytes 1500000 | tf_op jit(solution)/shard_map/unstack/pallas_call | solution.py:49
  (269 shorter events, 107.1 us)
Async XLA Ops:
  0.6 29.3 %collective-permute-start = (bf16[768,768]{1,0:T(8,128)(2,1)}, bf16[768,768]{1,0:T(8,128)(2,1)}, u32[]{:S(2)}, u32[]{:S(2)}) collective-permute-start(bf16[768,768]{1,0:T(8,128)(2,1)} %refs_0_.5), channel_id=1, source_target_pairs={{0,1},{1,0},{2,3},{3,2},{4,5},{5,4},{6,7},{7,6},{8,9},{9,8},{10,11... | collective-permute-start | bytes 3538952 | tf_op jit(solution)/shard_map/ppermute | solution.py:898
  30.0 14.3 %collective-permute-start.3 = (bf16[272,768]{1,0:T(8,128)(2,1)S(1)}, bf16[272,768]{1,0:T(8,128)(2,1)}, u32[]{:S(2)}, u32[]{:S(2)}) collective-permute-start(bf16[272,768]{1,0:T(8,128)(2,1)S(1)} %slice.52), channel_id=1, source_target_pairs={{0,1},{1,0},{2,3},{3,2},{4,5},{5,4},{6,7},{7,6},{8,9},{9,8},{10,11... | collective-permute-start | bytes 1253384 | tf_op jit(solution)/shard_map/ppermute | solution.py:898
  31.8 24.0 %collective-permute-start.7 = (bf16[256,768]{1,0:T(8,128)(2,1)S(1)}, bf16[256,768]{1,0:T(8,128)(2,1)}, u32[]{:S(2)}, u32[]{:S(2)}) collective-permute-start(bf16[256,768]{1,0:T(8,128)(2,1)S(1)} %slice.53), channel_id=1, source_target_pairs={{0,1},{1,0},{2,3},{3,2},{4,5},{5,4},{6,7},{7,6},{8,9},{9,8},{10,11... | collective-permute-start | bytes 1179656 | tf_op jit(solution)/shard_map/ppermute | solution.py:898
  44.2 13.8 %collective-permute-start.4 = (bf16[272,768]{1,0:T(8,128)(2,1)}, bf16[272,768]{1,0:T(8,128)(2,1)}, u32[]{:S(2)}, u32[]{:S(2)}) collective-permute-start(bf16[272,768]{1,0:T(8,128)(2,1)} %collective-permute-done.3.refs_1_), channel_id=1, source_target_pairs={{0,4},{2,6},{4,0},{6,2},{8,12},{10,14},{12,8},{14,10},{16,20},{18,... | collective-permute-start | bytes 1253384 | tf_op jit(solution)/shard_map/ppermute | solution.py:901
  55.8 18.1 %collective-permute-start.8 = (bf16[256,768]{1,0:T(8,128)(2,1)}, bf16[256,768]{1,0:T(8,128)(2,1)}, u32[]{:S(2)}, u32[]{:S(2)}) collective-permute-start(bf16[256,768]{1,0:T(8,128)(2,1)} %collective-permute-done.7.refs_5_), channel_id=1, source_target_pairs={{0,4},{2,6},{4,0},{6,2},{8,12},{10,14},{12,8},{14,10},{16,20},{18,... | collective-permute-start | bytes 1179656 | tf_op jit(solution)/shard_map/ppermute | solution.py:901
  56.1 18.0 %collective-permute-start.9 = (bf16[256,768]{1,0:T(8,128)(2,1)}, bf16[256,768]{1,0:T(8,128)(2,1)}, u32[]{:S(2)}, u32[]{:S(2)}) collective-permute-start(bf16[256,768]{1,0:T(8,128)(2,1)} %collective-permute-done.7.refs_5_), channel_id=1, source_target_pairs={{0,2},{2,0},{4,6},{6,4},{8,10},{10,8},{12,14},{14,12},{16,18},{18,... | collective-permute-start | bytes 1179656 | tf_op jit(solution)/shard_map/ppermute | solution.py:901
  56.1 19.8 %collective-permute-start.1 = (bf16[768,256]{1,0:T(8,128)(2,1)}, bf16[768,256]{1,0:T(8,128)(2,1)}, u32[]{:S(2)}, u32[]{:S(2)}) collective-permute-start(bf16[768,256]{1,0:T(8,128)(2,1)} %copy-done.38), channel_id=1, source_target_pairs={{0,1},{1,0},{2,3},{3,2},{4,5},{5,4},{6,7},{7,6},{8,9},{9,8},{10,11... | collective-permute-start | bytes 1179656 | tf_op jit(solution)/shard_map/ppermute | solution.py:898
  57.9 18.1 %collective-permute-start.5 = (bf16[272,768]{1,0:T(8,128)(2,1)}, bf16[272,768]{1,0:T(8,128)(2,1)}, u32[]{:S(2)}, u32[]{:S(2)}) collective-permute-start(bf16[272,768]{1,0:T(8,128)(2,1)} %collective-permute-done.3.refs_1_), channel_id=1, source_target_pairs={{0,2},{2,0},{4,6},{6,4},{8,10},{10,8},{12,14},{14,12},{16,18},{18,... | collective-permute-start | bytes 1253384 | tf_op jit(solution)/shard_map/ppermute | solution.py:901
  58.1 17.9 %collective-permute-start.6 = (bf16[272,768]{1,0:T(8,128)(2,1)}, bf16[272,768]{1,0:T(8,128)(2,1)}, u32[]{:S(2)}, u32[]{:S(2)}) collective-permute-start(bf16[272,768]{1,0:T(8,128)(2,1)} %collective-permute-done.4.refs_2_), channel_id=1, source_target_pairs={{0,2},{2,0},{4,6},{6,4},{8,10},{10,8},{12,14},{14,12},{16,18},{18,... | collective-permute-start | bytes 1253384 | tf_op jit(solution)/shard_map/ppermute | solution.py:901
  102.0 10.6 %collective-permute-start.11 = (bf16[768,256]{1,0:T(8,128)(2,1)S(1)}, bf16[768,256]{1,0:T(8,128)(2,1)S(1)}, u32[]{:S(2)}, u32[]{:S(2)}) collective-permute-start(bf16[768,256]{1,0:T(8,128)(2,1)S(1)} %get-tuple-element.126), channel_id=1, source_target_pairs={{0,1},{1,0},{2,3},{3,2},{4,5},{5,4},{6,7},{7,6},{8,9},{9,8},{10,11... | collective-permute-start | bytes 1179656 | tf_op jit(solution)/shard_map/ppermute | solution.py:898
  119.5 21.1 %collective-permute-start.15 = (bf16[2,272,768]{2,1,0:T(8,128)(2,1)}, bf16[2,272,768]{2,1,0:T(8,128)(2,1)S(1)}, u32[]{:S(2)}, u32[]{:S(2)}) collective-permute-start(bf16[2,272,768]{2,1,0:T(8,128)(2,1)} %get-tuple-element.143), channel_id=1, source_target_pairs={{0,4},{2,6},{4,0},{6,2},{8,12},{10,14},{12,8},{14,10},{16,20},{18,... | collective-permute-start | bytes 2506760 | tf_op jit(solution)/shard_map/ppermute | solution.py:901
  121.0 19.6 %collective-permute-start.14 = (bf16[512,768]{1,0:T(8,128)(2,1)}, bf16[512,768]{1,0:T(8,128)(2,1)}, u32[]{:S(2)}, u32[]{:S(2)}) collective-permute-start(bf16[512,768]{1,0:T(8,128)(2,1)} %get-tuple-element.137.refs_13_), channel_id=1, source_target_pairs={{0,1},{1,0},{2,3},{3,2},{4,5},{5,4},{6,7},{7,6},{8,9},{9,8},{10,11... | collective-permute-start | bytes 2359304 | tf_op jit(solution)/shard_map/ppermute | solution.py:898
  144.1 15.7 %collective-permute-start.17 = (bf16[272,768]{1,0:T(8,128)(2,1)}, bf16[272,768]{1,0:T(8,128)(2,1)}, u32[]{:S(2)}, u32[]{:S(2)}) collective-permute-start(bf16[272,768]{1,0:T(8,128)(2,1)} %get-tuple-element.149), channel_id=1, source_target_pairs={{0,1},{1,0},{2,3},{3,2},{4,5},{5,4},{6,7},{7,6},{8,9},{9,8},{10,11... | collective-permute-start | bytes 1253384 | tf_op jit(solution)/shard_map/ppermute | solution.py:898
  147.8 12.1 %collective-permute-start.16 = (bf16[256,768]{1,0:T(8,128)(2,1)}, bf16[256,768]{1,0:T(8,128)(2,1)}, u32[]{:S(2)}, u32[]{:S(2)}) collective-permute-start(bf16[256,768]{1,0:T(8,128)(2,1)} %get-tuple-element.147), channel_id=1, source_target_pairs={{0,4},{2,6},{4,0},{6,2},{8,12},{10,14},{12,8},{14,10},{16,20},{18,... | collective-permute-start | bytes 1179656 | tf_op jit(solution)/shard_map/ppermute | solution.py:901
  163.2 18.7 %collective-permute-start.20 = (bf16[272,768]{1,0:T(8,128)(2,1)S(1)}, bf16[272,768]{1,0:T(8,128)(2,1)S(1)}, u32[]{:S(2)}, u32[]{:S(2)}) collective-permute-start(bf16[272,768]{1,0:T(8,128)(2,1)S(1)} %get-tuple-element.155), channel_id=1, source_target_pairs={{0,8},{2,10},{4,12},{6,14},{8,0},{10,2},{12,4},{14,6},{16,24},{18,... | collective-permute-start | bytes 1253384 | tf_op jit(solution)/shard_map/ppermute | solution.py:901
  182.0 23.8 %collective-permute-start.22 = (bf16[272,768]{1,0:T(8,128)(2,1)S(1)}, bf16[272,768]{1,0:T(8,128)(2,1)S(1)}, u32[]{:S(2)}, u32[]{:S(2)}) collective-permute-start(bf16[272,768]{1,0:T(8,128)(2,1)S(1)} %plus.6.refs_12_.refs_0_), channel_id=1, source_target_pairs={{0,16},{2,18},{4,20},{6,22},{8,24},{10,26},{12,28},{14,30},{16,0},... | collective-permute-start | bytes 1253384 | tf_op jit(solution)/shard_map/ppermute | solution.py:901
  185.6 23.8 %collective-permute-start.23 = (bf16[192,768]{1,0:T(8,128)(2,1)S(1)}, bf16[192,768]{1,0:T(8,128)(2,1)S(1)}, u32[]{:S(2)}, u32[]{:S(2)}) collective-permute-start(bf16[192,768]{1,0:T(8,128)(2,1)S(1)} %get-tuple-element.158.refs_13_), channel_id=1, source_target_pairs={{0,4},{2,6},{4,0},{6,2},{8,12},{10,14},{12,8},{14,10},{16,20},{18,... | collective-permute-start | bytes 884744 | tf_op jit(solution)/shard_map/ppermute | solution.py:901
  208.9 14.5 %collective-permute-start.32 = (bf16[272,768]{1,0:T(8,128)(2,1)}, bf16[272,768]{1,0:T(8,128)(2,1)}, u32[]{:S(2)}, u32[]{:S(2)}) collective-permute-start(bf16[272,768]{1,0:T(8,128)(2,1)} %plus.7.refs_3_), channel_id=1, source_target_pairs={{0,8},{2,10},{4,12},{6,14},{8,0},{10,2},{12,4},{14,6},{16,24},{18,... | collective-permute-start | bytes 1253384 | tf_op jit(solution)/shard_map/ppermute | solution.py:901
  215.8 15.5 %collective-permute-start.25 = (bf16[384,768]{1,0:T(8,128)(2,1)}, bf16[384,768]{1,0:T(8,128)(2,1)S(1)}, u32[]{:S(2)}, u32[]{:S(2)}) collective-permute-start(bf16[384,768]{1,0:T(8,128)(2,1)} %get-tuple-element.187), channel_id=1, source_target_pairs={{0,1},{1,0},{2,3},{3,2},{4,5},{5,4},{6,7},{7,6},{8,9},{9,8},{10,11... | collective-permute-start | bytes 1769480 | tf_op jit(solution)/shard_map/ppermute | solution.py:898
  231.4 20.7 %collective-permute-start.33 = (bf16[544,768]{1,0:T(8,128)(2,1)}, bf16[544,768]{1,0:T(8,128)(2,1)S(1)}, u32[]{:S(2)}, u32[]{:S(2)}) collective-permute-start(bf16[544,768]{1,0:T(8,128)(2,1)} %pad_maximum_fusion.1), channel_id=1, source_target_pairs={{0,4},{2,6},{4,0},{6,2},{8,12},{10,14},{12,8},{14,10},{16,20},{18,... | collective-permute-start | bytes 2506760 | tf_op jit(solution)/shard_map/ppermute | solution.py:901
  239.8 12.3 %collective-permute-start.31 = (bf16[160,768]{1,0:T(8,128)(2,1)S(1)}, bf16[160,768]{1,0:T(8,128)(2,1)S(1)}, u32[]{:S(2)}, u32[]{:S(2)}) collective-permute-start(bf16[160,768]{1,0:T(8,128)(2,1)S(1)} %plus.8.refs_0_), channel_id=1, source_target_pairs={{0,16},{2,18},{4,20},{6,22},{8,24},{10,26},{12,28},{14,30},{16,0},... | collective-permute-start | bytes 737288 | tf_op jit(solution)/shard_map/ppermute | solution.py:901
  242.4 13.4 %collective-permute-start.30 = (bf16[384,768]{1,0:T(8,128)(2,1)}, bf16[384,768]{1,0:T(8,128)(2,1)S(1)}, u32[]{:S(2)}, u32[]{:S(2)}) collective-permute-start(bf16[384,768]{1,0:T(8,128)(2,1)} %get-tuple-element.172), channel_id=1, source_target_pairs={{0,1},{1,0},{2,3},{3,2},{4,5},{5,4},{6,7},{7,6},{8,9},{9,8},{10,11... | collective-permute-start | bytes 1769480 | tf_op jit(solution)/shard_map/ppermute | solution.py:898
  253.9 16.3 %collective-permute-start.37 = (bf16[1056,768]{1,0:T(8,128)(2,1)S(1)}, bf16[1056,768]{1,0:T(8,128)(2,1)S(1)}, u32[]{:S(2)}, u32[]{:S(2)}) collective-permute-start(bf16[1056,768]{1,0:T(8,128)(2,1)S(1)} %pad_maximum_fusion.refs_1_), channel_id=1, source_target_pairs={{0,2},{2,0},{4,6},{6,4},{8,10},{10,8},{12,14},{14,12},{16,18},{18,... | collective-permute-start | bytes 4866056 | tf_op jit(solution)/shard_map/ppermute | solution.py:901
  259.1 10.9 %collective-permute-start.36 = (bf16[288,768]{1,0:T(8,128)(2,1)S(1)}, bf16[288,768]{1,0:T(8,128)(2,1)S(1)}, u32[]{:S(2)}, u32[]{:S(2)}) collective-permute-start(bf16[288,768]{1,0:T(8,128)(2,1)S(1)} %pad_maximum_fusion.3), channel_id=1, source_target_pairs={{0,4},{2,6},{4,0},{6,2},{8,12},{10,14},{12,8},{14,10},{16,20},{18,... | collective-permute-start | bytes 1327112 | tf_op jit(solution)/shard_map/ppermute | solution.py:901
  (92 other events, 503.8 us)

commit v2 on v1

--- a/solution.py
+++ b/solution.py
@@ -249,10 +249,11 @@
     line = lax.broadcasted_iota(jnp.int32, (PAIR, rows), 0)
     tag = jnp.zeros((PAIR, rows), f32)
     mixed = []
-    for head in (0, 1):
-        q_in = jnp.where(lanes_of(head, q.shape), q, fq)
-        k_in = jnp.where(lanes_of(head, k.shape), k, fk)
-        score = nt(k_in, q_in)
+    scores = [
+        nt(jnp.where(lanes_of(n, k.shape), k, fk), jnp.where(lanes_of(n, q.shape), q, fq))
+        for n in (0, 1)
+    ]
+    for head, score in enumerate(scores):
         top = jnp.max(score, axis=0, keepdims=True)
         expo = jnp.exp(score - top)
         total = jnp.sum(expo, axis=0, keepdims=True)
@@ -353,15 +354,15 @@
     ones = jnp.where(
         jnp.logical_and(slot >= NSEG, slot < NSEG + 3), 1.0, 0.0
     ).astype(bf16)
-    dks, dvs = [], []
-    for head, qe_ref, de_ref in ((0, qa_ref, da_ref), (1, qb_ref, db_ref)):
-        mine = lanes_of(head, k.shape)
-        probs = jnp.exp(nt(jnp.where(mine, k, fk), qe_ref[...]))
-        dvs.append(nn(probs.astype(bf16), dol))
-        ds = (probs * nt(jnp.where(mine, v, ones), de_ref[...])).astype(bf16)
-        dks.append(nn(ds, q))
-        at = head * HD
-        dqt_ref[at : at + HD] += nn(k_turned[at : at + HD], ds)
+    heads = ((0, qa_ref, da_ref), (1, qb_ref, db_ref))
+    scores = [nt(jnp.where(lanes_of(h, k.shape), k, fk), a[...]) for h, a, b in heads]
+    grads = [nt(jnp.where(lanes_of(h, v.shape), v, ones), b[...]) for h, a, b in heads]
+    probs = [jnp.exp(s) for s in scores]
+    dvs = [nn(p.astype(bf16), dol) for p in probs]
+    dss = [(p * g).astype(bf16) for p, g in zip(probs, grads)]
+    dks = [nn(s, q) for s in dss]
+    for h in (0, 1):
+        dqt_ref[h * HD : h * HD + HD] += nn(k_turned[h * HD : h * HD + HD], dss[h])
     first = lanes_of(0, k.shape)
     rows = pl.ds(pl.multiple_of((step + start) * KBLK, KBLK), KBLK)
     dk = turn(jnp.where(first, dks[0], dks[1]), cos_ref[rows], sin_ref[rows], True).astype(bf16)

time: 284 us -> 282 us (level)
  transfers between devices with their start and end apart: 39 -> 39, of which waited for: 16 -> 16; matrix products, arithmetic and copies ran while one was open for 2% -> 2% of each run, Pallas kernels for 41% -> 40%
where the time goes in v2:
time: 282 us; the launch traced here: 278 us
  Pallas kernels  143 us (51%)
  waiting for transfers between devices  56.7 us (20%)
  local copies, waits for them, and re-layouts  36.7 us (13%)
  starting transfers between devices  36.2 us (13%)
  other arithmetic  3.68 us (1%)
    pallas_call x31, Pallas kernels, call(): pl.pallas_call(run, in_specs=list(in_specs) + [pl.BlockSpec(memory_space=...  119 us
    unnamed x154, local copies, waits for them, and re-layouts  33.6 us
    ppermute x27, waiting for transfers between devices, over(): return lax.ppermute(x, 'dp', [(n, n ^ bit) for n in range(dp)])  30.4 us
    ppermute x12, waiting for transfers between devices, over_y(): return lax.ppermute(x, 'tensor', [(0, 1), (1, 0)])  26.2 us
    ppermute x27, starting transfers between devices, over(): return lax.ppermute(x, 'dp', [(n, n ^ bit) for n in range(dp)])  21.9 us
    pallas_call x3, Pallas kernels, attend(): pl.pallas_call(attend_body, grid=(2,), in_specs=[pl.BlockSpec((rows, PAIR...  21.6 us
    ppermute x12, starting transfers between devices, over_y(): return lax.ppermute(x, 'tensor', [(0, 1), (1, 0)])  14.4 us
  transfers between devices with their start and end apart: 39, of which 16 were waited for; matrix products, arithmetic and copies ran while one was open for 2% of the time, Pallas kernels for 40%

profile of v2, /device:TPU:0, one launch (start us, length us, event | category | flops | bytes accessed | tf_op | source)
XLA Modules:
  0.0 278.0 jit_solution(732840518021638175)
XLA Ops:
  0.6 3.0 %collective-permute-start = (bf16[768,768]{1,0:T(8,128)(2,1)}, bf16[768,768]{1,0:T(8,128)(2,1)}, u32[]{:S(2)}, u32[]{:S(2)}) collective-permute-start(bf16[768,768]{1,0:T(8,128)(2,1)} %refs_0_.5), channel_id=1, source_target_pairs={{0,1},{1,0},{2,3},{3,2},{4,5},{5,4},{6,7},{7,6},{8,9},{9,8},{10,11... | collective-permute-start | bytes 3538952 | tf_op jit(solution)/shard_map/ppermute | solution.py:899
  16.6 2.9 %qkv.2 = (bf16[1536,768]{1,0:T(8,128)(2,1)S(1)}, bf16[1536,384]{1,0:T(8,128)(2,1)S(1)}, bf16[1536,384]{1,0:T(8,128)(2,1)S(1)}, bf16[1536,384]{1,0:T(8,128)(2,1)S(1)}) custom-call(bf16[768,768]{1,0:T(8,128)(2,1)S(1)} %copy-done.16, f32[1,768]{1,0:T(1,128)S(1)} %reshape.43.refs_1_, bf16[3,768,384]{2,1,0:T(8,128)(2,1)S(1)} %copy-done.7, ...), custom_call_target="tpu_custom_call" | custom-call | flops 407686336 | bytes 1800000 | tf_op jit(solution)/shard_map/qkv/pallas_call | solution.py:49
  19.6 10.4 %collective-permute-done.refs_0_.refs_4_ = bf16[768,768]{1,0:T(8,128)(2,1)} collective-permute-done((bf16[768,768]{1,0:T(8,128)(2,1)}, bf16[768,768]{1,0:T(8,128)(2,1)}, u32[]{:S(2)}, u32[]{:S(2)}) %collective-permute-start) | collective-permute-done | bytes 1179680 | tf_op jit(solution)/shard_map/ppermute | solution.py:899
  32.2 3.8 %qkv.3 = (bf16[1536,768]{1,0:T(8,128)(2,1)S(1)}, bf16[1536,384]{1,0:T(8,128)(2,1)S(1)}, bf16[1536,384]{1,0:T(8,128)(2,1)S(1)}, bf16[1536,384]{1,0:T(8,128)(2,1)S(1)}) custom-call(bf16[768,768]{1,0:T(8,128)(2,1)} %collective-permute-done.refs_0_.refs_4_, ...), custom_call_target="tpu_custom_call", output_to_operand_aliasing={{0}: (5, {}), {1}: (6, {}), {2}: (7, {}), {3}: (8, {})} | custom-call | flops 407686336 | bytes 1800000 | tf_op jit(solution)/shard_map/qkv/pallas_call | solution.py:49
  36.0 6.9 %attend.3 = (bf16[768,384]{1,0:T(8,128)(2,1)S(1)}, bf16[768,256]{1,0:T(8,128)(2,1)S(1)}, bf16[1536,128]{1,0:T(8,128)(2,1)S(1)}, bf16[1536,128]{1,0:T(8,128)(2,1)S(1)}) custom-call(bf16[1536,384]{1,0:T(8,128)(2,1)S(1)} %get-tuple-element.106.q_ref.refs_2_, bf16[1536,384]{1,0:T(8,128)(2,1)S(1)} %get-tuple-element.107.k_ref.refs_3_, ...), custom_call_target="tpu_custom_call" | custom-call | flops 1449551488 | bytes 450000 | tf_op jit(solution)/shard_map/attend/pallas_call | solution.py:290
  45.4 6.9 %attend.4 = (bf16[768,384]{1,0:T(8,128)(2,1)S(1)}, bf16[768,256]{1,0:T(8,128)(2,1)S(1)}, bf16[1536,128]{1,0:T(8,128)(2,1)S(1)}, bf16[1536,128]{1,0:T(8,128)(2,1)S(1)}) custom-call(bf16[1536,384]{1,0:T(8,128)(2,1)S(1)} %get-tuple-element.106.q_ref.refs_2_, ...), custom_call_target="tpu_custom_call", output_to_operand_aliasing={{0}: (5, {}), {1}: (6, {})} | custom-call | flops 1449551488 | bytes 450000 | tf_op jit(solution)/shard_map/attend/pallas_call | solution.py:290
  62.1 7.7 %attend.5 = (bf16[768,384]{1,0:T(8,128)(2,1)S(1)}, bf16[768,128]{1,0:T(8,128)(2,1)}, bf16[1536,128]{1,0:T(8,128)(2,1)S(1)}, bf16[1536,128]{1,0:T(8,128)(2,1)S(1)}) custom-call(bf16[1536,384]{1,0:T(8,128)(2,1)S(1)} %copy-done.11, bf16[1536,384]{1,0:T(8,128)(2,1)S(1)} %copy-done.13, bf16[1536,384]{1,0:T(8,128)(2,1)S(1)} %copy-done.15, ...), custom_call_target="tpu_custom_call", output_to_operand_aliasing={{0}: (5, {})} | custom-call | flops 1449551488 | bytes 450000 | tf_op jit(solution)/shard_map/attend/pallas_call | solution.py:290
  74.2 2.8 assemble.1.refs_8_
  77.0 2.8 %collective-permute-done.2.refs_5_.refs_2_ = bf16[768,128]{1,0:T(8,128)(2,1)} collective-permute-done((bf16[768,128]{1,0:T(8,128)(2,1)}, bf16[768,128]{1,0:T(8,128)(2,1)}, u32[]{:S(2)}, u32[]{:S(2)}) %collective-permute-start.2) | collective-permute-done | bytes 196640 | tf_op jit(solution)/shard_map/ppermute | solution.py:899
  79.9 20.3 %mlp.1 = (bf16[768,768]{1,0:T(8,128)(2,1)}, bf16[768,768]{1,0:T(8,128)(2,1)S(1)}, bf16[768,768]{1,0:T(8,128)(2,1)S(1)}, f32[768,768]{1,0:T(8,128)S(1)}, bf16[768...) custom-call(s32[2]{0:T(128)S(1)} %pad_add_fusion.refs_0_, ...), custom_call_target="tpu_custom_call" | custom-call | flops 2989699840 | bytes 3600000 | tf_op jit(solution)/shard_map/mlp/pallas_call | solution.py:49
  100.6 5.1 %weight_grads.2 = (bf16[1056,768]{1,0:T(8,128)(2,1)S(1)}, bf16[1056,768]{1,0:T(8,128)(2,1)S(1)}) custom-call(s32[1]{0:T(128)} %bitcast.8.refs_0_, bf16[768,256]{1,0:T(8,128)(2,1)} %collective-permute-done.1.refs_9_.refs_4_.refs_1_, bf16[768,128]{1,0:T(8,128)(2,1)} %collective-permute-done.2.refs_5_.refs_2_, ...), custom_call_target="tpu_custom_call" | custom-call | flops 15000 | bytes 1500 | tf_op jit(solution)/shard_map/weight_grads/pallas_call | solution.py:49
  105.7 3.1 %weight_grads.3 = (bf16[1056,768]{1,0:T(8,128)(2,1)S(1)}, bf16[1056,768]{1,0:T(8,128)(2,1)S(1)}) custom-call(s32[1]{0:T(128)} %bitcast.8.refs_0_, bf16[768,384]{1,0:T(8,128)(2,1)S(1)} %copy-done.21, bf16[6,768,576]{2,1,0:T(8,128)(2,1)S(1)} %get-tuple-element.127.refs_3_.refs_2_, bf16[768,768]{1,0:T(8,128)(2,1)S(1)} %get-tuple-element.128.refs_4_.refs_3_, ...), custom_call_target="tpu_custom_call" | custom-call | flops 15000 | bytes 1500 | tf_op jit(solution)/shard_map/weight_grads/pallas_call | solution.py:49
  112.3 2.7 collective-permute-done.12.refs_2_
  120.0 16.7 %attend_back.4.refs_1_.refs_5_.refs_0_ = bf16[1536,384]{1,0:T(8,128)(2,1)} custom-call(bf16[1536,128]{1,0:T(8,128)(2,1)} %copy-done.68, bf16[1536,128]{1,0:T(8,128)(2,1)} %copy-done.69, bf16[1536,384]{1,0:T(8,128)(2,1)} %copy-done.10, bf16[1536,384]{1,0:T(8,128)(2,1)} %copy-done.12, bf16[1536,384]{1,0:T(8,128)(2,1)} %copy-done.14, ...), custom_call_target="tpu_custom_call" | custom-call | flops 3623878656 | bytes 900000 | tf_op jit(solution)/shard_map/attend_back/pallas_call | solution.py:49
  150.7 7.4 %attend_back.5 = (f32[128,1536]{1,0:T(8,128)}, bf16[512,256]{1,0:T(8,128)(2,1)}) custom-call(bf16[1536,128]{1,0:T(8,128)(2,1)} %copy-done.36, bf16[1536,128]{1,0:T(8,128)(2,1)} %copy-done.37, bf16[1536,384]{1,0:T(8,128)(2,1)} %copy-done.10, bf16[1536,384]{1,0:T(8,128)(2,1)} %copy-done.12, bf16[1536,384]{1,0:T(8,128)(2,1)} %copy-done.14, ...), custom_call_target="tpu_custom_call" | custom-call | flops 1207959552 | bytes 900000 | tf_op jit(solution)/shard_map/attend_back/pallas_call | solution.py:49
  163.0 13.0 %attend_back.6.refs_2_.refs_1_ = bf16[1536,384]{1,0:T(8,128)(2,1)} custom-call(bf16[1536,128]{1,0:T(8,128)(2,1)} %copy-done.36, bf16[1536,128]{1,0:T(8,128)(2,1)} %copy-done.37, bf16[1536,384]{1,0:T(8,128)(2,1)} %copy-done.10, bf16[1536,384]{1,0:T(8,128)(2,1)} %copy-done.12, bf16[1536,384]{1,0:T(8,128)(2,1)} %copy-done.14, bf16[1536,128]{1,0:T(8,128)(2,1)} %copy-done.35, ...), custom_call_target="tpu_custom_call" | custom-call | flops 2415919104 | bytes 900000 | tf_op jit(solution)/shard_map/attend_back/pallas_call | solution.py:49
  186.6 16.9 %attend_back.7.refs_2_.refs_1_ = bf16[1536,384]{1,0:T(8,128)(2,1)} custom-call(bf16[1536,128]{1,0:T(8,128)(2,1)} %copy-done.66, bf16[1536,128]{1,0:T(8,128)(2,1)} %copy-done.67, bf16[1536,384]{1,0:T(8,128)(2,1)} %copy-done.10, bf16[1536,384]{1,0:T(8,128)(2,1)} %copy-done.12, bf16[1536,384]{1,0:T(8,128)(2,1)} %copy-done.14, bf16[1536,128]{1,0:T(8,128)(2,1)} %copy-done.35, ...), custom_call_target="tpu_custom_call" | custom-call | flops 3623878656 | bytes 900000 | tf_op jit(solution)/shard_map/attend_back/pallas_call | solution.py:49
  209.1 3.4 %tail.2 = (bf16[768,768]{1,0:T(8,128)(2,1)S(1)}, f32[8,768]{1,0:T(8,128)S(1)}) custom-call(bf16[1536,384]{1,0:T(8,128)(2,1)S(1)} %copy-done.3, bf16[1536,384]{1,0:T(8,128)(2,1)S(1)} %copy-done.1, bf16[1536,384]{1,0:T(8,128)(2,1)S(1)} %copy-done.5, bf16[1152,768]{1,0:T(8,128)(2,1)S(1)} %copy-done.19, bf16[768,768]{1,0:T(8,128)(2,1)} %collective-permute-done.refs_0_.refs_4_, ...), custom_call_target="tpu_custom_call" | custom-call | flops 15000 | bytes 1500 | tf_op jit(solution)/shard_map/tail/pallas_call | solution.py:49
  225.5 3.5 %collective-permute-done.25.refs_7_.refs_3_ = bf16[384,768]{1,0:T(8,128)(2,1)S(1)} collective-permute-done((bf16[384,768]{1,0:T(8,128)(2,1)}, bf16[384,768]{1,0:T(8,128)(2,1)S(1)}, u32[]{:S(2)}, u32[]{:S(2)}) %collective-permute-start.25) | collective-permute-done | bytes 589856 | tf_op jit(solution)/shard_map/ppermute | solution.py:899
  232.0 5.5 %collective-permute-done.29.refs_1_ = bf16[160,768]{1,0:T(8,128)(2,1)S(1)} collective-permute-done((bf16[160,768]{1,0:T(8,128)(2,1)S(1)}, bf16[160,768]{1,0:T(8,128)(2,1)S(1)}, u32[]{:S(2)}, u32[]{:S(2)}) %collective-permute-start.29) | collective-permute-done | bytes 245792 | tf_op jit(solution)/shard_map/ppermute | solution.py:902
  241.5 8.4 %collective-permute-done.31.refs_1_ = bf16[160,768]{1,0:T(8,128)(2,1)S(1)} collective-permute-done((bf16[160,768]{1,0:T(8,128)(2,1)S(1)}, bf16[160,768]{1,0:T(8,128)(2,1)S(1)}, u32[]{:S(2)}, u32[]{:S(2)}) %collective-permute-start.31) | collective-permute-done | bytes 245792 | tf_op jit(solution)/shard_map/ppermute | solution.py:902
  253.8 2.7 last.1
  257.8 9.9 %collective-permute-done.36 = bf16[288,768]{1,0:T(8,128)(2,1)S(1)} collective-permute-done((bf16[288,768]{1,0:T(8,128)(2,1)S(1)}, bf16[288,768]{1,0:T(8,128)(2,1)S(1)}, u32[]{:S(2)}, u32[]{:S(2)}) %collective-permute-start.36) | collective-permute-done | bytes 442400 | tf_op jit(solution)/shard_map/ppermute | solution.py:902
  268.0 3.1 %unstack.1 = (f32[384,768]{1,0:T(8,128)}, f32[2,576,768]{2,1,0:T(8,128)}, f32[576,768]{1,0:T(8,128)}) custom-call(s32[1]{0:T(128)} %bitcast.8.refs_0_, bf16[1056,768]{1,0:T(8,128)(2,1)S(1)} %pad_maximum_fusion.refs_1_, bf16[1056,768]{1,0:T(8,128)(2,1)S(1)} %collective-permute-done.37.refs_2_), custom_call_target="tpu_custom_call" | custom-call | flops 15000000 | bytes 1500000 | tf_op jit(solution)/shard_map/unstack/pallas_call | solution.py:49
  (269 shorter events, 107.4 us)
Async XLA Ops:
  0.6 29.3 %collective-permute-start = (bf16[768,768]{1,0:T(8,128)(2,1)}, bf16[768,768]{1,0:T(8,128)(2,1)}, u32[]{:S(2)}, u32[]{:S(2)}) collective-permute-start(bf16[768,768]{1,0:T(8,128)(2,1)} %refs_0_.5), channel_id=1, source_target_pairs={{0,1},{1,0},{2,3},{3,2},{4,5},{5,4},{6,7},{7,6},{8,9},{9,8},{10,11... | collective-permute-start | bytes 3538952 | tf_op jit(solution)/shard_map/ppermute | solution.py:899
  30.0 13.7 %collective-permute-start.3 = (bf16[272,768]{1,0:T(8,128)(2,1)S(1)}, bf16[272,768]{1,0:T(8,128)(2,1)}, u32[]{:S(2)}, u32[]{:S(2)}) collective-permute-start(bf16[272,768]{1,0:T(8,128)(2,1)S(1)} %slice.52), channel_id=1, source_target_pairs={{0,1},{1,0},{2,3},{3,2},{4,5},{5,4},{6,7},{7,6},{8,9},{9,8},{10,11... | collective-permute-start | bytes 1253384 | tf_op jit(solution)/shard_map/ppermute | solution.py:899
  31.8 22.8 %collective-permute-start.7 = (bf16[256,768]{1,0:T(8,128)(2,1)S(1)}, bf16[256,768]{1,0:T(8,128)(2,1)}, u32[]{:S(2)}, u32[]{:S(2)}) collective-permute-start(bf16[256,768]{1,0:T(8,128)(2,1)S(1)} %slice.53), channel_id=1, source_target_pairs={{0,1},{1,0},{2,3},{3,2},{4,5},{5,4},{6,7},{7,6},{8,9},{9,8},{10,11... | collective-permute-start | bytes 1179656 | tf_op jit(solution)/shard_map/ppermute | solution.py:899
  43.7 13.3 %collective-permute-start.4 = (bf16[272,768]{1,0:T(8,128)(2,1)}, bf16[272,768]{1,0:T(8,128)(2,1)}, u32[]{:S(2)}, u32[]{:S(2)}) collective-permute-start(bf16[272,768]{1,0:T(8,128)(2,1)} %collective-permute-done.3.refs_1_), channel_id=1, source_target_pairs={{0,4},{2,6},{4,0},{6,2},{8,12},{10,14},{12,8},{14,10},{16,20},{18,... | collective-permute-start | bytes 1253384 | tf_op jit(solution)/shard_map/ppermute | solution.py:902
  54.6 17.5 %collective-permute-start.8 = (bf16[256,768]{1,0:T(8,128)(2,1)}, bf16[256,768]{1,0:T(8,128)(2,1)}, u32[]{:S(2)}, u32[]{:S(2)}) collective-permute-start(bf16[256,768]{1,0:T(8,128)(2,1)} %collective-permute-done.7.refs_5_), channel_id=1, source_target_pairs={{0,4},{2,6},{4,0},{6,2},{8,12},{10,14},{12,8},{14,10},{16,20},{18,... | collective-permute-start | bytes 1179656 | tf_op jit(solution)/shard_map/ppermute | solution.py:902
  54.9 17.4 %collective-permute-start.9 = (bf16[256,768]{1,0:T(8,128)(2,1)}, bf16[256,768]{1,0:T(8,128)(2,1)}, u32[]{:S(2)}, u32[]{:S(2)}) collective-permute-start(bf16[256,768]{1,0:T(8,128)(2,1)} %collective-permute-done.7.refs_5_), channel_id=1, source_target_pairs={{0,2},{2,0},{4,6},{6,4},{8,10},{10,8},{12,14},{14,12},{16,18},{18,... | collective-permute-start | bytes 1179656 | tf_op jit(solution)/shard_map/ppermute | solution.py:902
  55.0 19.2 %collective-permute-start.1 = (bf16[768,256]{1,0:T(8,128)(2,1)}, bf16[768,256]{1,0:T(8,128)(2,1)}, u32[]{:S(2)}, u32[]{:S(2)}) collective-permute-start(bf16[768,256]{1,0:T(8,128)(2,1)} %copy-done.38), channel_id=1, source_target_pairs={{0,1},{1,0},{2,3},{3,2},{4,5},{5,4},{6,7},{7,6},{8,9},{9,8},{10,11... | collective-permute-start | bytes 1179656 | tf_op jit(solution)/shard_map/ppermute | solution.py:899
  56.8 17.5 %collective-permute-start.5 = (bf16[272,768]{1,0:T(8,128)(2,1)}, bf16[272,768]{1,0:T(8,128)(2,1)}, u32[]{:S(2)}, u32[]{:S(2)}) collective-permute-start(bf16[272,768]{1,0:T(8,128)(2,1)} %collective-permute-done.3.refs_1_), channel_id=1, source_target_pairs={{0,2},{2,0},{4,6},{6,4},{8,10},{10,8},{12,14},{14,12},{16,18},{18,... | collective-permute-start | bytes 1253384 | tf_op jit(solution)/shard_map/ppermute | solution.py:902
  56.9 17.3 %collective-permute-start.6 = (bf16[272,768]{1,0:T(8,128)(2,1)}, bf16[272,768]{1,0:T(8,128)(2,1)}, u32[]{:S(2)}, u32[]{:S(2)}) collective-permute-start(bf16[272,768]{1,0:T(8,128)(2,1)} %collective-permute-done.4.refs_2_), channel_id=1, source_target_pairs={{0,2},{2,0},{4,6},{6,4},{8,10},{10,8},{12,14},{14,12},{16,18},{18,... | collective-permute-start | bytes 1253384 | tf_op jit(solution)/shard_map/ppermute | solution.py:902
  100.2 10.6 %collective-permute-start.11 = (bf16[768,256]{1,0:T(8,128)(2,1)S(1)}, bf16[768,256]{1,0:T(8,128)(2,1)S(1)}, u32[]{:S(2)}, u32[]{:S(2)}) collective-permute-start(bf16[768,256]{1,0:T(8,128)(2,1)S(1)} %get-tuple-element.126), channel_id=1, source_target_pairs={{0,1},{1,0},{2,3},{3,2},{4,5},{5,4},{6,7},{7,6},{8,9},{9,8},{10,11... | collective-permute-start | bytes 1179656 | tf_op jit(solution)/shard_map/ppermute | solution.py:899
  117.7 21.1 %collective-permute-start.15 = (bf16[2,272,768]{2,1,0:T(8,128)(2,1)}, bf16[2,272,768]{2,1,0:T(8,128)(2,1)S(1)}, u32[]{:S(2)}, u32[]{:S(2)}) collective-permute-start(bf16[2,272,768]{2,1,0:T(8,128)(2,1)} %get-tuple-element.143), channel_id=1, source_target_pairs={{0,4},{2,6},{4,0},{6,2},{8,12},{10,14},{12,8},{14,10},{16,20},{18,... | collective-permute-start | bytes 2506760 | tf_op jit(solution)/shard_map/ppermute | solution.py:902
  119.2 19.6 %collective-permute-start.14 = (bf16[512,768]{1,0:T(8,128)(2,1)}, bf16[512,768]{1,0:T(8,128)(2,1)}, u32[]{:S(2)}, u32[]{:S(2)}) collective-permute-start(bf16[512,768]{1,0:T(8,128)(2,1)} %get-tuple-element.137.refs_13_), channel_id=1, source_target_pairs={{0,1},{1,0},{2,3},{3,2},{4,5},{5,4},{6,7},{7,6},{8,9},{9,8},{10,11... | collective-permute-start | bytes 2359304 | tf_op jit(solution)/shard_map/ppermute | solution.py:899
  142.4 15.8 %collective-permute-start.17 = (bf16[272,768]{1,0:T(8,128)(2,1)}, bf16[272,768]{1,0:T(8,128)(2,1)}, u32[]{:S(2)}, u32[]{:S(2)}) collective-permute-start(bf16[272,768]{1,0:T(8,128)(2,1)} %get-tuple-element.149), channel_id=1, source_target_pairs={{0,1},{1,0},{2,3},{3,2},{4,5},{5,4},{6,7},{7,6},{8,9},{9,8},{10,11... | collective-permute-start | bytes 1253384 | tf_op jit(solution)/shard_map/ppermute | solution.py:899
  146.0 12.1 %collective-permute-start.16 = (bf16[256,768]{1,0:T(8,128)(2,1)}, bf16[256,768]{1,0:T(8,128)(2,1)}, u32[]{:S(2)}, u32[]{:S(2)}) collective-permute-start(bf16[256,768]{1,0:T(8,128)(2,1)} %get-tuple-element.147), channel_id=1, source_target_pairs={{0,4},{2,6},{4,0},{6,2},{8,12},{10,14},{12,8},{14,10},{16,20},{18,... | collective-permute-start | bytes 1179656 | tf_op jit(solution)/shard_map/ppermute | solution.py:902
  161.5 18.5 %collective-permute-start.20 = (bf16[272,768]{1,0:T(8,128)(2,1)S(1)}, bf16[272,768]{1,0:T(8,128)(2,1)S(1)}, u32[]{:S(2)}, u32[]{:S(2)}) collective-permute-start(bf16[272,768]{1,0:T(8,128)(2,1)S(1)} %get-tuple-element.155), channel_id=1, source_target_pairs={{0,8},{2,10},{4,12},{6,14},{8,0},{10,2},{12,4},{14,6},{16,24},{18,... | collective-permute-start | bytes 1253384 | tf_op jit(solution)/shard_map/ppermute | solution.py:902
  180.1 23.5 %collective-permute-start.22 = (bf16[272,768]{1,0:T(8,128)(2,1)S(1)}, bf16[272,768]{1,0:T(8,128)(2,1)S(1)}, u32[]{:S(2)}, u32[]{:S(2)}) collective-permute-start(bf16[272,768]{1,0:T(8,128)(2,1)S(1)} %plus.6.refs_12_.refs_0_), channel_id=1, source_target_pairs={{0,16},{2,18},{4,20},{6,22},{8,24},{10,26},{12,28},{14,30},{16,0},... | collective-permute-start | bytes 1253384 | tf_op jit(solution)/shard_map/ppermute | solution.py:902
  183.6 23.5 %collective-permute-start.23 = (bf16[192,768]{1,0:T(8,128)(2,1)S(1)}, bf16[192,768]{1,0:T(8,128)(2,1)S(1)}, u32[]{:S(2)}, u32[]{:S(2)}) collective-permute-start(bf16[192,768]{1,0:T(8,128)(2,1)S(1)} %get-tuple-element.158.refs_13_), channel_id=1, source_target_pairs={{0,4},{2,6},{4,0},{6,2},{8,12},{10,14},{12,8},{14,10},{16,20},{18,... | collective-permute-start | bytes 884744 | tf_op jit(solution)/shard_map/ppermute | solution.py:902
  206.7 14.5 %collective-permute-start.32 = (bf16[272,768]{1,0:T(8,128)(2,1)}, bf16[272,768]{1,0:T(8,128)(2,1)}, u32[]{:S(2)}, u32[]{:S(2)}) collective-permute-start(bf16[272,768]{1,0:T(8,128)(2,1)} %plus.7.refs_3_), channel_id=1, source_target_pairs={{0,8},{2,10},{4,12},{6,14},{8,0},{10,2},{12,4},{14,6},{16,24},{18,... | collective-permute-start | bytes 1253384 | tf_op jit(solution)/shard_map/ppermute | solution.py:902
  213.5 15.5 %collective-permute-start.25 = (bf16[384,768]{1,0:T(8,128)(2,1)}, bf16[384,768]{1,0:T(8,128)(2,1)S(1)}, u32[]{:S(2)}, u32[]{:S(2)}) collective-permute-start(bf16[384,768]{1,0:T(8,128)(2,1)} %get-tuple-element.187), channel_id=1, source_target_pairs={{0,1},{1,0},{2,3},{3,2},{4,5},{5,4},{6,7},{7,6},{8,9},{9,8},{10,11... | collective-permute-start | bytes 1769480 | tf_op jit(solution)/shard_map/ppermute | solution.py:899
  229.2 20.6 %collective-permute-start.33 = (bf16[544,768]{1,0:T(8,128)(2,1)}, bf16[544,768]{1,0:T(8,128)(2,1)S(1)}, u32[]{:S(2)}, u32[]{:S(2)}) collective-permute-start(bf16[544,768]{1,0:T(8,128)(2,1)} %pad_maximum_fusion.1), channel_id=1, source_target_pairs={{0,4},{2,6},{4,0},{6,2},{8,12},{10,14},{12,8},{14,10},{16,20},{18,... | collective-permute-start | bytes 2506760 | tf_op jit(solution)/shard_map/ppermute | solution.py:902
  237.6 12.3 %collective-permute-start.31 = (bf16[160,768]{1,0:T(8,128)(2,1)S(1)}, bf16[160,768]{1,0:T(8,128)(2,1)S(1)}, u32[]{:S(2)}, u32[]{:S(2)}) collective-permute-start(bf16[160,768]{1,0:T(8,128)(2,1)S(1)} %plus.8.refs_0_), channel_id=1, source_target_pairs={{0,16},{2,18},{4,20},{6,22},{8,24},{10,26},{12,28},{14,30},{16,0},... | collective-permute-start | bytes 737288 | tf_op jit(solution)/shard_map/ppermute | solution.py:902
  240.2 13.4 %collective-permute-start.30 = (bf16[384,768]{1,0:T(8,128)(2,1)}, bf16[384,768]{1,0:T(8,128)(2,1)S(1)}, u32[]{:S(2)}, u32[]{:S(2)}) collective-permute-start(bf16[384,768]{1,0:T(8,128)(2,1)} %get-tuple-element.172), channel_id=1, source_target_pairs={{0,1},{1,0},{2,3},{3,2},{4,5},{5,4},{6,7},{7,6},{8,9},{9,8},{10,11... | collective-permute-start | bytes 1769480 | tf_op jit(solution)/shard_map/ppermute | solution.py:899
  251.6 16.3 %collective-permute-start.37 = (bf16[1056,768]{1,0:T(8,128)(2,1)S(1)}, bf16[1056,768]{1,0:T(8,128)(2,1)S(1)}, u32[]{:S(2)}, u32[]{:S(2)}) collective-permute-start(bf16[1056,768]{1,0:T(8,128)(2,1)S(1)} %pad_maximum_fusion.refs_1_), channel_id=1, source_target_pairs={{0,2},{2,0},{4,6},{6,4},{8,10},{10,8},{12,14},{14,12},{16,18},{18,... | collective-permute-start | bytes 4866056 | tf_op jit(solution)/shard_map/ppermute | solution.py:902
  256.8 10.9 %collective-permute-start.36 = (bf16[288,768]{1,0:T(8,128)(2,1)S(1)}, bf16[288,768]{1,0:T(8,128)(2,1)S(1)}, u32[]{:S(2)}, u32[]{:S(2)}) collective-permute-start(bf16[288,768]{1,0:T(8,128)(2,1)S(1)} %pad_maximum_fusion.3), channel_id=1, source_target_pairs={{0,4},{2,6},{4,0},{6,2},{8,12},{10,14},{12,8},{14,10},{16,20},{18,... | collective-permute-start | bytes 1327112 | tf_op jit(solution)/shard_map/ppermute | solution.py:902
  (92 other events, 498.7 us)

commit v3 on v2

--- a/solution.py
+++ b/solution.py
@@ -13,7 +13,7 @@
 PAIR = 2 * HD
 BLK = 384
 MLP_BLK = 256
-COST = 0.15
+COST = 0.12
 KBLK = 512
 rope_theta = 160000.0
 norm_eps = 1e-05

time: 282 us -> 277 us (0.982)
  Pallas kernels: 143 us -> 139 us
  waiting for transfers between devices: 56.7 us -> 60 us
    pallas_call x31, Pallas kernels: 119 us -> 115 us  [call(): pl.pallas_call(run, in_specs=list(in_specs) + [pl.BlockSpec(memory_space=...]
    unnamed x154 -> x158, local copies, waits for them, and re-layouts: 33.6 us -> 32 us
where the time goes in v3:
time: 277 us; the launch traced here: 273 us
  Pallas kernels  139 us (50%)
  waiting for transfers between devices  60 us (22%)
  local copies, waits for them, and re-layouts  35 us (13%)
  starting transfers between devices  34.2 us (12%)
  other arithmetic  3.54 us (1%)
    pallas_call x31, Pallas kernels, call(): pl.pallas_call(run, in_specs=list(in_specs) + [pl.BlockSpec(memory_space=...  115 us
    ppermute x27, waiting for transfers between devices, over(): return lax.ppermute(x, 'dp', [(n, n ^ bit) for n in range(dp)])  32.1 us
    unnamed x158, local copies, waits for them, and re-layouts  32 us
    ppermute x12, waiting for transfers between devices, over_y(): return lax.ppermute(x, 'tensor', [(0, 1), (1, 0)])  27.9 us
    pallas_call x3, Pallas kernels, attend(): pl.pallas_call(attend_body, grid=(2,), in_specs=[pl.BlockSpec((rows, PAIR...  21.8 us
    ppermute x27, starting transfers between devices, over(): return lax.ppermute(x, 'dp', [(n, n ^ bit) for n in range(dp)])  20.6 us
    ppermute x12, starting transfers between devices, over_y(): return lax.ppermute(x, 'tensor', [(0, 1), (1, 0)])  13.6 us
  transfers between devices with their start and end apart: 39, of which 16 were waited for; matrix products, arithmetic and copies ran while one was open for 2% of the time, Pallas kernels for 40%

profile of v3, /device:TPU:0, one launch (start us, length us, event | category | flops | bytes accessed | tf_op | source)
XLA Modules:
  0.0 273.3 jit_solution(2663066451385050704)
XLA Ops:
  0.6 3.0 %collective-permute-start = (bf16[768,768]{1,0:T(8,128)(2,1)}, bf16[768,768]{1,0:T(8,128)(2,1)}, u32[]{:S(2)}, u32[]{:S(2)}) collective-permute-start(bf16[768,768]{1,0:T(8,128)(2,1)} %refs_0_.5), channel_id=1, source_target_pairs={{0,1},{1,0},{2,3},{3,2},{4,5},{5,4},{6,7},{7,6},{8,9},{9,8},{10,11... | collective-permute-start | bytes 3538952 | tf_op jit(solution)/shard_map/ppermute | solution.py:899
  16.7 2.9 %qkv.2 = (bf16[1536,768]{1,0:T(8,128)(2,1)S(1)}, bf16[1536,384]{1,0:T(8,128)(2,1)S(1)}, bf16[1536,384]{1,0:T(8,128)(2,1)S(1)}, bf16[1536,384]{1,0:T(8,128)(2,1)S(1)}) custom-call(bf16[768,768]{1,0:T(8,128)(2,1)S(1)} %copy-done.15, f32[1,768]{1,0:T(1,128)S(1)} %reshape.43.refs_1_, bf16[3,768,384]{2,1,0:T(8,128)(2,1)S(1)} %copy-done.21, ...), custom_call_target="tpu_custom_call" | custom-call | flops 326149088 | bytes 1440000 | tf_op jit(solution)/shard_map/qkv/pallas_call | solution.py:49
  19.7 10.3 %collective-permute-done.refs_0_.refs_4_ = bf16[768,768]{1,0:T(8,128)(2,1)} collective-permute-done((bf16[768,768]{1,0:T(8,128)(2,1)}, bf16[768,768]{1,0:T(8,128)(2,1)}, u32[]{:S(2)}, u32[]{:S(2)}) %collective-permute-start) | collective-permute-done | bytes 1179680 | tf_op jit(solution)/shard_map/ppermute | solution.py:899
  32.2 3.8 %qkv.3 = (bf16[1536,768]{1,0:T(8,128)(2,1)S(1)}, bf16[1536,384]{1,0:T(8,128)(2,1)S(1)}, bf16[1536,384]{1,0:T(8,128)(2,1)S(1)}, bf16[1536,384]{1,0:T(8,128)(2,1)S(1)}) custom-call(bf16[768,768]{1,0:T(8,128)(2,1)} %collective-permute-done.refs_0_.refs_4_, ...), custom_call_target="tpu_custom_call", output_to_operand_aliasing={{0}: (5, {}), {1}: (6, {}), {2}: (7, {}), {3}: (8, {})} | custom-call | flops 326149088 | bytes 1440000 | tf_op jit(solution)/shard_map/qkv/pallas_call | solution.py:49
  37.4 7.0 %attend.3 = (bf16[768,384]{1,0:T(8,128)(2,1)S(1)}, bf16[768,256]{1,0:T(8,128)(2,1)S(1)}, bf16[1536,128]{1,0:T(8,128)(2,1)S(1)}, bf16[1536,128]{1,0:T(8,128)(2,1)S(1)}) custom-call(bf16[1536,384]{1,0:T(8,128)(2,1)S(1)} %get-tuple-element.106.q_ref.refs_2_, bf16[1536,384]{1,0:T(8,128)(2,1)S(1)} %get-tuple-element.107.k_ref.refs_3_, ...), custom_call_target="tpu_custom_call" | custom-call | flops 1159641216 | bytes 360000 | tf_op jit(solution)/shard_map/attend/pallas_call | solution.py:290
  47.7 7.0 %attend.4 = (bf16[768,384]{1,0:T(8,128)(2,1)S(1)}, bf16[768,256]{1,0:T(8,128)(2,1)S(1)}, bf16[1536,128]{1,0:T(8,128)(2,1)S(1)}, bf16[1536,128]{1,0:T(8,128)(2,1)S(1)}) custom-call(bf16[1536,384]{1,0:T(8,128)(2,1)S(1)} %get-tuple-element.106.q_ref.refs_2_, ...), custom_call_target="tpu_custom_call", output_to_operand_aliasing={{0}: (5, {}), {1}: (6, {})} | custom-call | flops 1159641216 | bytes 360000 | tf_op jit(solution)/shard_map/attend/pallas_call | solution.py:290
  63.5 7.8 %attend.5 = (bf16[768,384]{1,0:T(8,128)(2,1)S(1)}, bf16[768,128]{1,0:T(8,128)(2,1)}, bf16[1536,128]{1,0:T(8,128)(2,1)S(1)}, bf16[1536,128]{1,0:T(8,128)(2,1)S(1)}) custom-call(bf16[1536,384]{1,0:T(8,128)(2,1)S(1)} %get-tuple-element.106.q_ref.refs_2_, bf16[1536,384]{1,0:T(8,128)(2,1)S(1)} %get-tuple-element.107.k_ref.refs_3_, ...), custom_call_target="tpu_custom_call", output_to_operand_aliasing={{0}: (5, {})} | custom-call | flops 1159641216 | bytes 360000 | tf_op jit(solution)/shard_map/attend/pallas_call | solution.py:290
  78.4 2.8 %collective-permute-done.2.refs_5_.refs_2_ = bf16[768,128]{1,0:T(8,128)(2,1)S(1)} collective-permute-done((bf16[768,128]{1,0:T(8,128)(2,1)}, bf16[768,128]{1,0:T(8,128)(2,1)S(1)}, u32[]{:S(2)}, u32[]{:S(2)}) %collective-permute-start.2) | collective-permute-done | bytes 196640 | tf_op jit(solution)/shard_map/ppermute | solution.py:899
  81.3 20.8 %mlp.1 = (bf16[768,768]{1,0:T(8,128)(2,1)}, bf16[768,768]{1,0:T(8,128)(2,1)S(1)}, bf16[768,768]{1,0:T(8,128)(2,1)S(1)}, f32[768,768]{1,0:T(8,128)S(1)}, bf16[768...) custom-call(s32[2]{0:T(128)S(1)} %pad_add_fusion.refs_0_, ...), custom_call_target="tpu_custom_call" | custom-call | flops 2391759872 | bytes 2880000 | tf_op jit(solution)/shard_map/mlp/pallas_call | solution.py:49
  102.4 4.8 %weight_grads.2 = (bf16[1056,768]{1,0:T(8,128)(2,1)S(1)}, bf16[1056,768]{1,0:T(8,128)(2,1)S(1)}) custom-call(s32[1]{0:T(128)} %bitcast.8.refs_0_, bf16[768,256]{1,0:T(8,128)(2,1)} %collective-permute-done.1.refs_9_.refs_4_.refs_1_, bf16[768,128]{1,0:T(8,128)(2,1)S(1)} %collective-permute-done.2.refs_5_.refs_2_, ...), custom_call_target="tpu_custom_call" | custom-call | flops 12000 | bytes 1200 | tf_op jit(solution)/shard_map/weight_grads/pallas_call | solution.py:49
  107.3 3.1 %weight_grads.3 = (bf16[1056,768]{1,0:T(8,128)(2,1)S(1)}, bf16[1056,768]{1,0:T(8,128)(2,1)S(1)}) custom-call(s32[1]{0:T(128)} %bitcast.8.refs_0_, bf16[768,384]{1,0:T(8,128)(2,1)S(1)} %copy-done.12, bf16[6,768,576]{2,1,0:T(8,128)(2,1)S(1)} %get-tuple-element.127.refs_3_.refs_2_, bf16[768,768]{1,0:T(8,128)(2,1)S(1)} %get-tuple-element.128.refs_4_.refs_3_, ...), custom_call_target="tpu_custom_call" | custom-call | flops 12000 | bytes 1200 | tf_op jit(solution)/shard_map/weight_grads/pallas_call | solution.py:49
  121.0 16.7 %attend_back.4.refs_1_.refs_5_.refs_0_ = bf16[1536,384]{1,0:T(8,128)(2,1)} custom-call(bf16[1536,128]{1,0:T(8,128)(2,1)} %copy-done.60, bf16[1536,128]{1,0:T(8,128)(2,1)} %copy-done.61, bf16[1536,384]{1,0:T(8,128)(2,1)} %copy-done, bf16[1536,384]{1,0:T(8,128)(2,1)} %copy-done.1, bf16[1536,384]{1,0:T(8,128)(2,1)} %copy-done.2, bf16[1536,128]{1,0:T(8,128)(2,1)} %copy-done.22, ...), custom_call_target="tpu_custom_call" | custom-call | flops 2899102976 | bytes 720000 | tf_op jit(solution)/shard_map/attend_back/pallas_call | solution.py:49
  146.9 7.5 %attend_back.5 = (f32[128,1536]{1,0:T(8,128)}, bf16[512,256]{1,0:T(8,128)(2,1)}) custom-call(bf16[1536,128]{1,0:T(8,128)(2,1)} %copy-done.46, bf16[1536,128]{1,0:T(8,128)(2,1)} %copy-done.47, bf16[1536,384]{1,0:T(8,128)(2,1)} %copy-done, bf16[1536,384]{1,0:T(8,128)(2,1)} %copy-done.1, bf16[1536,384]{1,0:T(8,128)(2,1)} %copy-done.2, ...), custom_call_target="tpu_custom_call" | custom-call | flops 966367616 | bytes 720000 | tf_op jit(solution)/shard_map/attend_back/pallas_call | solution.py:49
  158.2 12.9 %attend_back.6.refs_2_.refs_1_ = bf16[1536,384]{1,0:T(8,128)(2,1)} custom-call(bf16[1536,128]{1,0:T(8,128)(2,1)} %copy-done.46, bf16[1536,128]{1,0:T(8,128)(2,1)} %copy-done.47, bf16[1536,384]{1,0:T(8,128)(2,1)} %copy-done, bf16[1536,384]{1,0:T(8,128)(2,1)} %copy-done.1, bf16[1536,384]{1,0:T(8,128)(2,1)} %copy-done.2, bf16[1536,128]{1,0:T(8,128)(2,1)} %copy-done.22, ...), custom_call_target="tpu_custom_call" | custom-call | flops 1932735232 | bytes 720000 | tf_op jit(solution)/shard_map/attend_back/pallas_call | solution.py:49
  181.8 17.0 %attend_back.7.refs_2_.refs_1_ = bf16[1536,384]{1,0:T(8,128)(2,1)} custom-call(bf16[1536,128]{1,0:T(8,128)(2,1)} %copy-done.64, bf16[1536,128]{1,0:T(8,128)(2,1)} %copy-done.65, bf16[1536,384]{1,0:T(8,128)(2,1)} %copy-done, bf16[1536,384]{1,0:T(8,128)(2,1)} %copy-done.1, bf16[1536,384]{1,0:T(8,128)(2,1)} %copy-done.2, bf16[1536,128]{1,0:T(8,128)(2,1)} %copy-done.22, ...), custom_call_target="tpu_custom_call" | custom-call | flops 2899102976 | bytes 720000 | tf_op jit(solution)/shard_map/attend_back/pallas_call | solution.py:49
  203.8 3.4 %tail.2 = (bf16[768,768]{1,0:T(8,128)(2,1)S(1)}, f32[8,768]{1,0:T(8,128)S(1)}) custom-call(bf16[1536,384]{1,0:T(8,128)(2,1)S(1)} %copy-done.8, bf16[1536,384]{1,0:T(8,128)(2,1)S(1)} %copy-done.6, bf16[1536,384]{1,0:T(8,128)(2,1)S(1)} %copy-done.19, bf16[1152,768]{1,0:T(8,128)(2,1)S(1)} %copy-done.25, bf16[768,768]{1,0:T(8,128)(2,1)} %collective-permute-done.refs_0_.refs_4_, ...), custom_call_target="tpu_custom_call" | custom-call | flops 12000 | bytes 1200 | tf_op jit(solution)/shard_map/tail/pallas_call | solution.py:49
  219.7 4.1 %collective-permute-done.25.refs_7_.refs_3_ = bf16[384,768]{1,0:T(8,128)(2,1)S(1)} collective-permute-done((bf16[384,768]{1,0:T(8,128)(2,1)S(1)}, bf16[384,768]{1,0:T(8,128)(2,1)S(1)}, u32[]{:S(2)}, u32[]{:S(2)}) %collective-permute-start.25) | collective-permute-done | bytes 589856 | tf_op jit(solution)/shard_map/ppermute | solution.py:899
  225.7 6.3 %collective-permute-done.29.refs_1_ = bf16[160,768]{1,0:T(8,128)(2,1)S(1)} collective-permute-done((bf16[160,768]{1,0:T(8,128)(2,1)S(1)}, bf16[160,768]{1,0:T(8,128)(2,1)S(1)}, u32[]{:S(2)}, u32[]{:S(2)}) %collective-permute-start.29) | collective-permute-done | bytes 245792 | tf_op jit(solution)/shard_map/ppermute | solution.py:902
  232.1 2.7 collective-permute-start.31
  235.6 9.1 %collective-permute-done.31.refs_1_ = bf16[160,768]{1,0:T(8,128)(2,1)S(1)} collective-permute-done((bf16[160,768]{1,0:T(8,128)(2,1)S(1)}, bf16[160,768]{1,0:T(8,128)(2,1)S(1)}, u32[]{:S(2)}, u32[]{:S(2)}) %collective-permute-start.31) | collective-permute-done | bytes 245792 | tf_op jit(solution)/shard_map/ppermute | solution.py:902
  248.4 2.7 last.1
  253.7 9.4 %collective-permute-done.36 = bf16[288,768]{1,0:T(8,128)(2,1)S(1)} collective-permute-done((bf16[288,768]{1,0:T(8,128)(2,1)S(1)}, bf16[288,768]{1,0:T(8,128)(2,1)S(1)}, u32[]{:S(2)}, u32[]{:S(2)}) %collective-permute-start.36) | collective-permute-done | bytes 442400 | tf_op jit(solution)/shard_map/ppermute | solution.py:902
  263.3 3.2 %unstack.1 = (f32[384,768]{1,0:T(8,128)}, f32[2,576,768]{2,1,0:T(8,128)}, f32[576,768]{1,0:T(8,128)}) custom-call(s32[1]{0:T(128)} %bitcast.8.refs_0_, bf16[1056,768]{1,0:T(8,128)(2,1)S(1)} %pad_maximum_fusion.refs_1_, bf16[1056,768]{1,0:T(8,128)(2,1)S(1)} %collective-permute-done.37.refs_2_), custom_call_target="tpu_custom_call" | custom-call | flops 12000000 | bytes 1200000 | tf_op jit(solution)/shard_map/unstack/pallas_call | solution.py:49
  267.4 2.7 collective-permute-done.35
  (273 shorter events, 100.6 us)
Async XLA Ops:
  0.6 29.3 %collective-permute-start = (bf16[768,768]{1,0:T(8,128)(2,1)}, bf16[768,768]{1,0:T(8,128)(2,1)}, u32[]{:S(2)}, u32[]{:S(2)}) collective-permute-start(bf16[768,768]{1,0:T(8,128)(2,1)} %refs_0_.5), channel_id=1, source_target_pairs={{0,1},{1,0},{2,3},{3,2},{4,5},{5,4},{6,7},{7,6},{8,9},{9,8},{10,11... | collective-permute-start | bytes 3538952 | tf_op jit(solution)/shard_map/ppermute | solution.py:899
  30.0 16.0 %collective-permute-start.3 = (bf16[272,768]{1,0:T(8,128)(2,1)S(1)}, bf16[272,768]{1,0:T(8,128)(2,1)}, u32[]{:S(2)}, u32[]{:S(2)}) collective-permute-start(bf16[272,768]{1,0:T(8,128)(2,1)S(1)} %slice.52), channel_id=1, source_target_pairs={{0,1},{1,0},{2,3},{3,2},{4,5},{5,4},{6,7},{7,6},{8,9},{9,8},{10,11... | collective-permute-start | bytes 1253384 | tf_op jit(solution)/shard_map/ppermute | solution.py:899
  31.8 26.0 %collective-permute-start.7 = (bf16[256,768]{1,0:T(8,128)(2,1)S(1)}, bf16[256,768]{1,0:T(8,128)(2,1)}, u32[]{:S(2)}, u32[]{:S(2)}) collective-permute-start(bf16[256,768]{1,0:T(8,128)(2,1)S(1)} %slice.53), channel_id=1, source_target_pairs={{0,1},{1,0},{2,3},{3,2},{4,5},{5,4},{6,7},{7,6},{8,9},{9,8},{10,11... | collective-permute-start | bytes 1179656 | tf_op jit(solution)/shard_map/ppermute | solution.py:899
  46.0 14.1 %collective-permute-start.4 = (bf16[272,768]{1,0:T(8,128)(2,1)}, bf16[272,768]{1,0:T(8,128)(2,1)}, u32[]{:S(2)}, u32[]{:S(2)}) collective-permute-start(bf16[272,768]{1,0:T(8,128)(2,1)} %collective-permute-done.3.refs_1_), channel_id=1, source_target_pairs={{0,4},{2,6},{4,0},{6,2},{8,12},{10,14},{12,8},{14,10},{16,20},{18,... | collective-permute-start | bytes 1253384 | tf_op jit(solution)/shard_map/ppermute | solution.py:902
  57.8 15.8 %collective-permute-start.8 = (bf16[256,768]{1,0:T(8,128)(2,1)}, bf16[256,768]{1,0:T(8,128)(2,1)}, u32[]{:S(2)}, u32[]{:S(2)}) collective-permute-start(bf16[256,768]{1,0:T(8,128)(2,1)} %collective-permute-done.7.refs_5_), channel_id=1, source_target_pairs={{0,4},{2,6},{4,0},{6,2},{8,12},{10,14},{12,8},{14,10},{16,20},{18,... | collective-permute-start | bytes 1179656 | tf_op jit(solution)/shard_map/ppermute | solution.py:902
  58.1 15.7 %collective-permute-start.9 = (bf16[256,768]{1,0:T(8,128)(2,1)}, bf16[256,768]{1,0:T(8,128)(2,1)}, u32[]{:S(2)}, u32[]{:S(2)}) collective-permute-start(bf16[256,768]{1,0:T(8,128)(2,1)} %collective-permute-done.7.refs_5_), channel_id=1, source_target_pairs={{0,2},{2,0},{4,6},{6,4},{8,10},{10,8},{12,14},{14,12},{16,18},{18,... | collective-permute-start | bytes 1179656 | tf_op jit(solution)/shard_map/ppermute | solution.py:902
  58.1 17.6 %collective-permute-start.1 = (bf16[768,256]{1,0:T(8,128)(2,1)}, bf16[768,256]{1,0:T(8,128)(2,1)}, u32[]{:S(2)}, u32[]{:S(2)}) collective-permute-start(bf16[768,256]{1,0:T(8,128)(2,1)} %copy-done.26), channel_id=1, source_target_pairs={{0,1},{1,0},{2,3},{3,2},{4,5},{5,4},{6,7},{7,6},{8,9},{9,8},{10,11... | collective-permute-start | bytes 1179656 | tf_op jit(solution)/shard_map/ppermute | solution.py:899
  59.9 15.8 %collective-permute-start.5 = (bf16[272,768]{1,0:T(8,128)(2,1)}, bf16[272,768]{1,0:T(8,128)(2,1)}, u32[]{:S(2)}, u32[]{:S(2)}) collective-permute-start(bf16[272,768]{1,0:T(8,128)(2,1)} %collective-permute-done.3.refs_1_), channel_id=1, source_target_pairs={{0,2},{2,0},{4,6},{6,4},{8,10},{10,8},{12,14},{14,12},{16,18},{18,... | collective-permute-start | bytes 1253384 | tf_op jit(solution)/shard_map/ppermute | solution.py:902
  60.1 15.6 %collective-permute-start.6 = (bf16[272,768]{1,0:T(8,128)(2,1)}, bf16[272,768]{1,0:T(8,128)(2,1)}, u32[]{:S(2)}, u32[]{:S(2)}) collective-permute-start(bf16[272,768]{1,0:T(8,128)(2,1)} %collective-permute-done.4.refs_2_), channel_id=1, source_target_pairs={{0,2},{2,0},{4,6},{6,4},{8,10},{10,8},{12,14},{14,12},{16,18},{18,... | collective-permute-start | bytes 1253384 | tf_op jit(solution)/shard_map/ppermute | solution.py:902
  102.0 10.6 %collective-permute-start.11 = (bf16[768,256]{1,0:T(8,128)(2,1)S(1)}, bf16[768,256]{1,0:T(8,128)(2,1)S(1)}, u32[]{:S(2)}, u32[]{:S(2)}) collective-permute-start(bf16[768,256]{1,0:T(8,128)(2,1)S(1)} %get-tuple-element.126), channel_id=1, source_target_pairs={{0,1},{1,0},{2,3},{3,2},{4,5},{5,4},{6,7},{7,6},{8,9},{9,8},{10,11... | collective-permute-start | bytes 1179656 | tf_op jit(solution)/shard_map/ppermute | solution.py:899
  118.0 21.0 %collective-permute-start.15 = (bf16[2,272,768]{2,1,0:T(8,128)(2,1)S(1)}, bf16[2,272,768]{2,1,0:T(8,128)(2,1)S(1)}, u32[]{:S(2)}, u32[]{:S(2)}) collective-permute-start(bf16[2,272,768]{2,1,0:T(8,128)(2,1)S(1)} %get-tuple-element.143), channel_id=1, source_target_pairs={{0,4},{2,6},{4,0},{6,2},{8,12},{10,14},{12,8},{14,10},{16,20},{18,... | collective-permute-start | bytes 2506760 | tf_op jit(solution)/shard_map/ppermute | solution.py:902
  119.7 19.3 %collective-permute-start.14 = (bf16[512,768]{1,0:T(8,128)(2,1)S(1)}, bf16[512,768]{1,0:T(8,128)(2,1)S(1)}, u32[]{:S(2)}, u32[]{:S(2)}) collective-permute-start(bf16[512,768]{1,0:T(8,128)(2,1)S(1)} %get-tuple-element.137.refs_13_), channel_id=1, source_target_pairs={{0,1},{1,0},{2,3},{3,2},{4,5},{5,4},{6,7},{7,6},{8,9},{9,8},{10,11... | collective-permute-start | bytes 2359304 | tf_op jit(solution)/shard_map/ppermute | solution.py:899
  141.5 12.9 %collective-permute-start.17 = (bf16[272,768]{1,0:T(8,128)(2,1)}, bf16[272,768]{1,0:T(8,128)(2,1)S(1)}, u32[]{:S(2)}, u32[]{:S(2)}) collective-permute-start(bf16[272,768]{1,0:T(8,128)(2,1)} %get-tuple-element.149), channel_id=1, source_target_pairs={{0,1},{1,0},{2,3},{3,2},{4,5},{5,4},{6,7},{7,6},{8,9},{9,8},{10,11... | collective-permute-start | bytes 1253384 | tf_op jit(solution)/shard_map/ppermute | solution.py:899
  142.7 11.7 %collective-permute-start.16 = (bf16[256,768]{1,0:T(8,128)(2,1)}, bf16[256,768]{1,0:T(8,128)(2,1)S(1)}, u32[]{:S(2)}, u32[]{:S(2)}) collective-permute-start(bf16[256,768]{1,0:T(8,128)(2,1)} %get-tuple-element.147), channel_id=1, source_target_pairs={{0,4},{2,6},{4,0},{6,2},{8,12},{10,14},{12,8},{14,10},{16,20},{18,... | collective-permute-start | bytes 1179656 | tf_op jit(solution)/shard_map/ppermute | solution.py:902
  155.8 19.1 %collective-permute-start.20 = (bf16[272,768]{1,0:T(8,128)(2,1)S(1)}, bf16[272,768]{1,0:T(8,128)(2,1)S(1)}, u32[]{:S(2)}, u32[]{:S(2)}) collective-permute-start(bf16[272,768]{1,0:T(8,128)(2,1)S(1)} %get-tuple-element.155), channel_id=1, source_target_pairs={{0,8},{2,10},{4,12},{6,14},{8,0},{10,2},{12,4},{14,6},{16,24},{18,... | collective-permute-start | bytes 1253384 | tf_op jit(solution)/shard_map/ppermute | solution.py:902
  175.0 23.8 %collective-permute-start.22 = (bf16[272,768]{1,0:T(8,128)(2,1)S(1)}, bf16[272,768]{1,0:T(8,128)(2,1)S(1)}, u32[]{:S(2)}, u32[]{:S(2)}) collective-permute-start(bf16[272,768]{1,0:T(8,128)(2,1)S(1)} %plus.6.refs_12_.refs_0_), channel_id=1, source_target_pairs={{0,16},{2,18},{4,20},{6,22},{8,24},{10,26},{12,28},{14,30},{16,0},... | collective-permute-start | bytes 1253384 | tf_op jit(solution)/shard_map/ppermute | solution.py:902
  178.5 23.5 %collective-permute-start.23 = (bf16[192,768]{1,0:T(8,128)(2,1)S(1)}, bf16[192,768]{1,0:T(8,128)(2,1)S(1)}, u32[]{:S(2)}, u32[]{:S(2)}) collective-permute-start(bf16[192,768]{1,0:T(8,128)(2,1)S(1)} %get-tuple-element.158.refs_13_), channel_id=1, source_target_pairs={{0,4},{2,6},{4,0},{6,2},{8,12},{10,14},{12,8},{14,10},{16,20},{18,... | collective-permute-start | bytes 884744 | tf_op jit(solution)/shard_map/ppermute | solution.py:902
  201.3 14.0 %collective-permute-start.32 = (bf16[272,768]{1,0:T(8,128)(2,1)S(1)}, bf16[272,768]{1,0:T(8,128)(2,1)}, u32[]{:S(2)}, u32[]{:S(2)}) collective-permute-start(bf16[272,768]{1,0:T(8,128)(2,1)S(1)} %plus.7.refs_3_), channel_id=1, source_target_pairs={{0,8},{2,10},{4,12},{6,14},{8,0},{10,2},{12,4},{14,6},{16,24},{18,... | collective-permute-start | bytes 1253384 | tf_op jit(solution)/shard_map/ppermute | solution.py:902
  208.1 15.7 %collective-permute-start.25 = (bf16[384,768]{1,0:T(8,128)(2,1)S(1)}, bf16[384,768]{1,0:T(8,128)(2,1)S(1)}, u32[]{:S(2)}, u32[]{:S(2)}) collective-permute-start(bf16[384,768]{1,0:T(8,128)(2,1)S(1)} %get-tuple-element.187), channel_id=1, source_target_pairs={{0,1},{1,0},{2,3},{3,2},{4,5},{5,4},{6,7},{7,6},{8,9},{9,8},{10,11... | collective-permute-start | bytes 1769480 | tf_op jit(solution)/shard_map/ppermute | solution.py:899
  224.0 20.7 %collective-permute-start.33 = (bf16[544,768]{1,0:T(8,128)(2,1)}, bf16[544,768]{1,0:T(8,128)(2,1)S(1)}, u32[]{:S(2)}, u32[]{:S(2)}) collective-permute-start(bf16[544,768]{1,0:T(8,128)(2,1)} %pad_maximum_fusion.1), channel_id=1, source_target_pairs={{0,4},{2,6},{4,0},{6,2},{8,12},{10,14},{12,8},{14,10},{16,20},{18,... | collective-permute-start | bytes 2506760 | tf_op jit(solution)/shard_map/ppermute | solution.py:902
  232.1 12.6 %collective-permute-start.31 = (bf16[160,768]{1,0:T(8,128)(2,1)S(1)}, bf16[160,768]{1,0:T(8,128)(2,1)S(1)}, u32[]{:S(2)}, u32[]{:S(2)}) collective-permute-start(bf16[160,768]{1,0:T(8,128)(2,1)S(1)} %plus.8.refs_0_), channel_id=1, source_target_pairs={{0,16},{2,18},{4,20},{6,22},{8,24},{10,26},{12,28},{14,30},{16,0},... | collective-permute-start | bytes 737288 | tf_op jit(solution)/shard_map/ppermute | solution.py:902
  234.8 13.6 %collective-permute-start.30 = (bf16[384,768]{1,0:T(8,128)(2,1)}, bf16[384,768]{1,0:T(8,128)(2,1)S(1)}, u32[]{:S(2)}, u32[]{:S(2)}) collective-permute-start(bf16[384,768]{1,0:T(8,128)(2,1)} %get-tuple-element.172), channel_id=1, source_target_pairs={{0,1},{1,0},{2,3},{3,2},{4,5},{5,4},{6,7},{7,6},{8,9},{9,8},{10,11... | collective-permute-start | bytes 1769480 | tf_op jit(solution)/shard_map/ppermute | solution.py:899
  245.9 17.3 %collective-permute-start.37 = (bf16[1056,768]{1,0:T(8,128)(2,1)S(1)}, bf16[1056,768]{1,0:T(8,128)(2,1)S(1)}, u32[]{:S(2)}, u32[]{:S(2)}) collective-permute-start(bf16[1056,768]{1,0:T(8,128)(2,1)S(1)} %pad_maximum_fusion.refs_1_), channel_id=1, source_target_pairs={{0,2},{2,0},{4,6},{6,4},{8,10},{10,8},{12,14},{14,12},{16,18},{18,... | collective-permute-start | bytes 4866056 | tf_op jit(solution)/shard_map/ppermute | solution.py:902
  252.3 10.8 %collective-permute-start.36 = (bf16[288,768]{1,0:T(8,128)(2,1)S(1)}, bf16[288,768]{1,0:T(8,128)(2,1)S(1)}, u32[]{:S(2)}, u32[]{:S(2)}) collective-permute-start(bf16[288,768]{1,0:T(8,128)(2,1)S(1)} %pad_maximum_fusion.3), channel_id=1, source_target_pairs={{0,4},{2,6},{4,0},{6,2},{8,12},{10,14},{12,8},{14,10},{16,20},{18,... | collective-permute-start | bytes 1327112 | tf_op jit(solution)/shard_map/ppermute | solution.py:902
  (94 other events, 557.5 us)
